TPU v7x, 32 devices: a whole 2x2x4 slice. The times are simulated.
32 devices in a mesh: gx: 4 (over z), gy: 8 (over y, x, core).
Axes of the slice: x: 2, y: 2, z: 4, core: 2. Of those that a mesh axis runs over, the one named last changes fastest.
Arguments:
- a_tiles: float32 [256, 4, 128, 128], P(('gx', 'gy')), may hold values from -6 to 6
- a_cols: int32 [256, 4], P(('gx', 'gy')), may hold values from 0 to 255, as said below
- new_row: int32 [256], P(('gx', 'gy')), may hold values from 0 to 255, as said below
- p_tiles: float32 [256, 2, 128, 128], P(('gx', 'gy')), may hold values from -0.5 to 0.5
- p_cols: int32 [256, 2], P(('gx', 'gy')), may hold values from 0 to 63, as said below
Outputs:
- coarse: float32 [64, 10, 128, 128], P(('gx', 'gy'))
Inputs may be any that keep to these rules, and one draw needn't show every extreme that they name: A permutation; the new owner new_row // 8 of a block row has the same gy index as its old owner and a gx index 0 to 3 above the old owner's, modulo the number of gx indices; at most 2 block rows of one device go to one new owner. `a_cols`: the first column block of old block row o is new_row[o]; the others are distinct block rows of the devices with the same gx index as new_row[o]'s owner and gy index one below, equal or one above. `p_cols`: for block row g owned by device d (gy index y), the first coarse block is one of d's 2 coarse blocks, the second one of device d + 1's, or of d's where y is the last gy index.
All inputs are finite; a program needn't handle non-finite values.
Results may differ from a plain program's by a relative error of at most 0.0003.
Values sent between devices are 32-bit elements; how exact they have to be, the bound alone decides.
A program may use at most 128 MiB of HBM per device.

v0:
```python
import jax
import jax.numpy as jnp
from jax import lax
from jax.sharding import PartitionSpec as P

A_TILES = 4
P_TILES = 2
CAP = 2


def with_halo(shard, sides, width):
    for axis, dim in sides:
        size, length = (lax.axis_size(axis), shard.shape[dim])
        up = [(i, (i + 1) % size) for i in range(size - 1)]
        down = [(j, i) for i, j in up]
        last = lax.slice_in_dim(shard, length - width, length, axis=dim)
        leading = lax.slice_in_dim(shard, 0, width, axis=dim)
        before = lax.ppermute(last, axis, up)
        after = lax.ppermute(leading, axis, down)
        shard = jnp.concatenate([before, shard, after], axis=dim)
    return shard


def from_behind(block, axis, distance):
    devices = range(lax.axis_size(axis))
    route = [((i - distance) % len(devices), i) for i in devices]
    return lax.ppermute(block, axis, route)


def shifted(value, axis, steps):
    count = lax.axis_size(axis)
    leading, last = (max(0, -steps), min(count, count - steps))
    return lax.ppermute(value, axis, [(source, source + steps) for source in range(leading, last)])


def fetch_neighbours(p_tiles, p_cols, row_count):
    return (
        with_halo(p_tiles, (("gy", 0),), row_count),
        with_halo(p_cols.astype(jnp.float32), (("gy", 0),), row_count),
    )


def shards(a_tiles, a_cols, new_row, p_tiles, p_cols):
    row_count = a_tiles.shape[0]
    tile_size = a_tiles.shape[2]
    gx_count = lax.axis_size("gx")
    gy_count = lax.axis_size("gy")
    coarse_count = row_count // 4
    my_x = lax.axis_index("gx")
    device_id = my_x * gy_count + lax.axis_index("gy")
    target_x = new_row // row_count // gy_count
    new_local = new_row % row_count
    row_order = jnp.arange(row_count)
    earlier = (target_x[:, None] == target_x[None, :]) & (row_order[None, :] < row_order[:, None])
    rank_in_peer = jnp.sum(earlier.astype(jnp.int32), axis=1)
    span_count = min(6, gx_count)
    distance = (target_x - my_x) % gx_count
    bucket = distance * CAP + rank_in_peer
    send_tiles = (
        jnp.zeros((span_count * CAP,) + a_tiles.shape[1:], jnp.float32).at[bucket].set(a_tiles)
    )
    send_cols = (
        jnp.zeros((span_count * CAP, A_TILES), jnp.float32)
        .at[bucket]
        .set(a_cols.astype(jnp.float32))
    )
    send_dest = (
        jnp.full((span_count * CAP,), float(row_count), jnp.float32)
        .at[bucket]
        .set(new_local.astype(jnp.float32))
    )
    tile_parts = [send_tiles[:CAP]]
    col_parts = [send_cols[:CAP]]
    dest_parts = [send_dest[:CAP]]
    for step_by in range(1, span_count):
        lower = step_by * CAP
        came_tiles, came_cols, came_dest = from_behind(
            (
                send_tiles[lower : lower + CAP],
                send_cols[lower : lower + CAP],
                send_dest[lower : lower + CAP],
            ),
            "gx",
            step_by,
        )
        tile_parts.append(came_tiles)
        col_parts.append(came_cols)
        dest_parts.append(came_dest)
    got_tiles = jnp.concatenate(tile_parts, axis=0)
    got_cols = jnp.concatenate(col_parts, axis=0)
    got_dest = jnp.concatenate(dest_parts, axis=0)
    dest_slot = got_dest.astype(jnp.int32)
    moved = jnp.zeros_like(a_tiles).at[dest_slot].set(got_tiles, mode="drop")
    moved_cols = (
        jnp.zeros((row_count, A_TILES), jnp.int32)
        .at[dest_slot]
        .set(got_cols.astype(jnp.int32), mode="drop")
    )
    local_index = moved_cols - (device_id - 1) * row_count
    ext_tiles, ext_cols = fetch_neighbours(p_tiles, p_cols, row_count)
    fetched = ext_tiles[local_index]
    products = jnp.einsum("rkab,rkqbc->rkqac", moved, fetched, precision=lax.Precision.HIGHEST)
    targets = ext_cols.astype(jnp.int32)[local_index]
    wide_slot = targets - (device_id - 1) * coarse_count
    select = (wide_slot[:, None, :, :] == jnp.arange(4 * coarse_count)[None, :, None, None]).astype(
        jnp.float32
    )
    select = select.reshape(row_count, 4 * coarse_count, A_TILES * P_TILES)
    flat_products = products.reshape(row_count, A_TILES * P_TILES, tile_size, tile_size)
    summed = jnp.einsum("rsm,rmac->rsac", select, flat_products, precision=lax.Precision.HIGHEST)
    lifted = jnp.einsum("rpba,rsbc->rpsac", p_tiles, summed, precision=lax.Precision.HIGHEST)
    owner_slot = p_cols - device_id * coarse_count
    owner_pick = (owner_slot[None, :, :] == jnp.arange(2 * coarse_count)[:, None, None]).astype(
        jnp.float32
    )
    partial_value = jnp.einsum(
        "trp,rpsac->tsac", owner_pick, lifted, precision=lax.Precision.HIGHEST
    )
    zero_band = jnp.zeros((coarse_count, coarse_count, tile_size, tile_size), jnp.float32)
    own_rows = jnp.concatenate([zero_band, partial_value[:coarse_count]], axis=1)
    next_rows = jnp.concatenate([partial_value[coarse_count:], zero_band], axis=1)
    arrived = shifted(next_rows, "gy", 1)
    return own_rows + arrived


def solution(mesh):
    in_specs = (
        P(("gx", "gy"), None, None, None),
        P(("gx", "gy"), None),
        P(("gx", "gy")),
        P(("gx", "gy"), None, None, None),
        P(("gx", "gy"), None),
    )
    out_specs = P(("gx", "gy"), None, None, None)
    return jax.shard_map(shards, mesh=mesh, in_specs=in_specs, out_specs=out_specs, check_vma=False)
```

profile of v0, /device:TPU:12, one launch (start us, length us, event | category | flops | bytes accessed | tf_op | source)
XLA Modules:
  0.0 166.4 jit_solution(6542185666566068281)
XLA Ops:
  0.0 1.9 %collective-permute-start.8 = (f32[8,2,128,128]{3,2,1,0:T(8,128)}, f32[8,2,128,128]{3,2,1,0:T(8,128)}, u32[]{:S(2)}, u32[]{:S(2)}) collective-permute-start(f32[8,2,128,128]{3,2,1,0:T(8,128)} %param.8), channel_id=1, source_target_pairs={{0,1},{1,2},{2,3},{3,4},{4,5},{5,6},{6,7},{8,9},{9,10},{10,11},{11... | collective-permute-start | bytes 3145736 | tf_op jit(solution)/shard_map/ppermute | solution.py:18
  1.9 4.5 %collective-permute-start.9 = (f32[8,2,128,128]{3,2,1,0:T(8,128)}, f32[8,2,128,128]{3,2,1,0:T(8,128)}, u32[]{:S(2)}, u32[]{:S(2)}) collective-permute-start(f32[8,2,128,128]{3,2,1,0:T(8,128)} %param.8), channel_id=1, source_target_pairs={{1,0},{2,1},{3,2},{4,3},{5,4},{6,5},{7,6},{9,8},{10,9},{11,10},{12... | collective-permute-start | bytes 3145736 | tf_op jit(solution)/shard_map/ppermute | solution.py:19
  6.5 0.8 broadcast_subtract_fusion.1
  7.2 1.9 %collective-permute-start = (f32[8,2]{0,1:T(2,128)S(1)}, f32[8,2]{0,1:T(2,128)S(1)}, u32[]{:S(2)}, u32[]{:S(2)}) collective-permute-start(f32[8,2]{0,1:T(2,128)S(1)} %get-tuple-element.16), channel_id=1, source_target_pairs={{0,1},{1,2},{2,3},{3,4},{4,5},{5,6},{6,7},{8,9},{9,10},{10,11},{11... | collective-permute-start | bytes 200 | tf_op jit(solution)/shard_map/ppermute | solution.py:18
  9.2 4.5 %collective-permute-start.1 = (f32[8,2]{0,1:T(2,128)S(1)}, f32[8,2]{0,1:T(2,128)S(1)}, u32[]{:S(2)}, u32[]{:S(2)}) collective-permute-start(f32[8,2]{0,1:T(2,128)S(1)} %get-tuple-element.16), channel_id=1, source_target_pairs={{1,0},{2,1},{3,2},{4,3},{5,4},{6,5},{7,6},{9,8},{10,9},{11,10},{12... | collective-permute-start | bytes 200 | tf_op jit(solution)/shard_map/ppermute | solution.py:19
  13.7 0.7 fusion.27
  14.4 0.2 convert_reduce_fusion
  14.6 0.6 scatter_custom_fusion
  15.2 0.1 slice_bitcast_fusion
  15.3 1.6 collective-permute-start.2
  16.8 0.7 convert_element_type.35
  17.5 0.1 copy.27
  17.6 0.2 broadcast.79.clone
  17.8 2.5 %scatter_fusion = f32[8,4,128,128]{3,2,1,0:T(8,128)S(1)} fusion(f32[8,4,128,128]{3,2,1,0:T(8,128)S(1)} %broadcast.79.clone, s32[8]{0:T(128)S(1)} %compare_select_fusion.2, f32[8,4,128,128]{3,2,1,0:T(8,128)} %param.5), kind=kCustom, calls=%fused_computation.5 | custom fusion | bytes 6291488 | tf_op jit(solution)/shard_map/scatter | solution.py:60
  20.3 1.2 fusion.33
  21.5 0.6 scatter_custom_fusion.1
  22.1 0.0 collective-permute-done.2
  22.1 1.3 collective-permute-start.3
  23.4 3.2 %collective-permute-done.3 = f32[2]{0:T(128)S(1)} collective-permute-done((f32[2]{0:T(128)S(1)}, f32[2]{0:T(128)S(1)}, u32[]{:S(2)}, u32[]{:S(2)}) %collective-permute-start.3) | collective-permute-done | bytes 40 | tf_op jit(solution)/shard_map/ppermute | solution.py:27
  26.6 0.4 collective-permute-start.4
  27.1 3.1 %collective-permute-done.4 = f32[2]{0:T(128)S(1)} collective-permute-done((f32[2]{0:T(128)S(1)}, f32[2]{0:T(128)S(1)}, u32[]{:S(2)}, u32[]{:S(2)}) %collective-permute-start.4) | collective-permute-done | bytes 40 | tf_op jit(solution)/shard_map/ppermute | solution.py:27
  30.2 1.6 collective-permute-start.5
  31.8 0.1 fusion.29
  31.8 1.9 %collective-permute-done.5 = f32[2,4]{1,0:T(2,128)S(1)} collective-permute-done((f32[2,4]{1,0:T(2,128)S(1)}, f32[2,4]{1,0:T(2,128)S(1)}, u32[]{:S(2)}, u32[]{:S(2)}) %collective-permute-start.5) | collective-permute-done | bytes 64 | tf_op jit(solution)/shard_map/ppermute | solution.py:27
  33.8 3.0 %collective-permute-start.6 = (f32[2,4]{1,0:T(2,128)S(1)}, f32[2,4]{1,0:T(2,128)S(1)}, u32[]{:S(2)}, u32[]{:S(2)}) collective-permute-start(f32[2,4]{1,0:T(2,128)S(1)} %get-tuple-element.13), channel_id=1, source_target_pairs={{16,0},{24,8},{0,16},{8,24},{17,1},{25,9},{1,17},{9,25},{18,2},{26... | collective-permute-start | bytes 104 | tf_op jit(solution)/shard_map/ppermute | solution.py:27
  36.8 1.5 collective-permute-done.6
  38.3 2.4 %collective-permute-start.7 = (f32[2,4]{1,0:T(2,128)S(1)}, f32[2,4]{1,0:T(2,128)S(1)}, u32[]{:S(2)}, u32[]{:S(2)}) collective-permute-start(f32[2,4]{1,0:T(2,128)S(1)} %get-tuple-element.12), channel_id=1, source_target_pairs={{8,0},{16,8},{24,16},{0,24},{9,1},{17,9},{25,17},{1,25},{10,2},{18... | collective-permute-start | bytes 104 | tf_op jit(solution)/shard_map/ppermute | solution.py:27
  40.7 1.4 collective-permute-done.7
  42.0 1.5 collective-permute-start.10
  43.5 0.6 scatter_custom_fusion.2
  44.1 0.0 collective-permute-done
  44.1 3.4 %collective-permute-start.11 = (f32[2,4,128,128]{3,2,1,0:T(8,128)}, f32[2,4,128,128]{3,2,1,0:T(8,128)S(1)}, u32[]{:S(2)}, u32[]{:S(2)}) collective-permute-start(f32[2,4,128,128]{3,2,1,0:T(8,128)} %get-tuple-element.9), channel_id=1, source_target_pairs={{16,0},{24,8},{0,16},{8,24},{17,1},{25,9},{1,17},{9,25},{18,2},{26... | collective-permute-start | bytes 1572872 | tf_op jit(solution)/shard_map/ppermute | solution.py:27
  47.5 0.0 collective-permute-done.1
  47.5 2.0 %collective-permute-start.12 = (f32[2,4,128,128]{3,2,1,0:T(8,128)S(1)}, f32[2,4,128,128]{3,2,1,0:T(8,128)S(1)}, u32[]{:S(2)}, u32[]{:S(2)}) collective-permute-start(f32[2,4,128,128]{3,2,1,0:T(8,128)S(1)} %get-tuple-element.8), channel_id=1, source_target_pairs={{8,0},{16,8},{24,16},{0,24},{9,1},{17,9},{25,17},{1,25},{10,2},{18... | collective-permute-start | bytes 1572872 | tf_op jit(solution)/shard_map/ppermute | solution.py:27
  49.6 0.1 reshape.82
  49.7 0.1 maximum_convert_fusion.2
  49.7 0.1 copy.28
  49.8 0.6 gather_fusion
  50.4 0.1 sub.53
  50.5 25.4 %collective-permute-done.10 = f32[2,4,128,128]{3,2,1,0:T(8,128)S(1)} collective-permute-done((f32[2,4,128,128]{3,2,1,0:T(8,128)}, f32[2,4,128,128]{3,2,1,0:T(8,128)S(1)}, u32[]{:S(2)}, u32[]{:S(2)}) %collective-permute-start.10) | collective-permute-done | bytes 524320 | tf_op jit(solution)/shard_map/ppermute | solution.py:27
  75.9 5.6 %collective-permute-done.11 = f32[2,4,128,128]{3,2,1,0:T(8,128)S(1)} collective-permute-done((f32[2,4,128,128]{3,2,1,0:T(8,128)}, f32[2,4,128,128]{3,2,1,0:T(8,128)S(1)}, u32[]{:S(2)}, u32[]{:S(2)}) %collective-permute-start.11) | collective-permute-done | bytes 524320 | tf_op jit(solution)/shard_map/ppermute | solution.py:27
  81.6 3.7 %collective-permute-done.12 = f32[2,4,128,128]{3,2,1,0:T(8,128)S(1)} collective-permute-done((f32[2,4,128,128]{3,2,1,0:T(8,128)S(1)}, f32[2,4,128,128]{3,2,1,0:T(8,128)S(1)}, u32[]{:S(2)}, u32[]{:S(2)}) %collective-permute-start.12) | collective-permute-done | bytes 524320 | tf_op jit(solution)/shard_map/ppermute | solution.py:27
  85.2 1.6 pad_maximum_fusion.1
  86.8 0.2 broadcast.79
  87.0 0.0 copy-start
  87.0 2.5 %scatter_fusion.1 = f32[8,4,128,128]{3,2,1,0:T(8,128)S(1)} fusion(f32[8,4,128,128]{3,2,1,0:T(8,128)S(1)} %broadcast.79, s32[8]{0:T(128)S(1)} %fusion.29, f32[8,4,128,128]{3,2,1,0:T(8,128)} %pad_maximum_fusion.1), kind=kCustom, calls=%fused_computation.6 | custom fusion | bytes 6291488 | tf_op jit(solution)/shard_map/scatter | solution.py:93
  89.5 0.0 collective-permute-done.8
  89.5 0.0 collective-permute-done.9
  89.6 0.0 copy-done
  89.6 3.5 %pad_maximum_fusion = f32[24,2,128,128]{3,2,1,0:T(8,128)} fusion(f32[8,2,128,128]{3,2,1,0:T(8,128)} %collective-permute-done.9, f32[8,2,128,128]{3,2,1,0:T(8,128)S(1)} %copy-done, f32[8,2,128,128]{3,2,1,0:T(8,128)} %collective-permute-done.8), kind=kLoop, calls=%fused_computation.10 | loop fusion | flops 1572864 | bytes 6291456 | tf_op jit(solution)/shard_map/concatenate | solution.py:20
  93.1 4.6 %gather_fusion.1 = f32[32,2,128,128]{3,2,1,0:T(8,128)} fusion(f32[24,2,128,128]{3,2,1,0:T(8,128)} %pad_maximum_fusion, s32[1024]{0:T(1024)S(1)} %pad_clamp_fusion), kind=kCustom, calls=%fused_computation.1 | custom fusion | bytes 8388736 | tf_op jit(solution)/shard_map/gather | solution.py:101
  97.7 10.5 %fusion.5 = f32[8,4,2,128,128]{4,3,2,1,0:T(8,128)} fusion(f32[8,4,2,128,128]{4,3,2,1,0:T(8,128)} %bitcast.42, f32[8,4,128,128]{3,2,1,0:T(8,128)S(1)} %scatter_fusion.1), kind=kOutput, calls=%fused_computation.13 | convolution fusion | flops 1610612736 | bytes 10485760 | tf_op jit(solution)/shard_map/rkab,rkqbc->rkqac/dot_general | solution.py:102
  108.2 5.3 %copy.30 = f32[8,8,128,128]{3,1,2,0:T(8,128)} copy(f32[8,8,128,128]{2,3,1,0:T(8,128)} %bitcast.41) | data formatting | bytes 8388608 | tf_op jit(solution)/shard_map/reshape | solution.py:109
  113.5 4.3 %convolution_bitcast_fusion = f32[8,8,128,128,1]{3,1,2,0,4:T(8,128)S(1)} fusion(f32[8,8,128,128]{3,1,2,0:T(8,128)} %copy.30, s32[8,8]{1,0:T(8,128)S(1)} %sub.53), kind=kOutput, calls=%fused_computation.11 | convolution fusion | flops 100663808 | bytes 8388864 | tf_op jit(solution)/shard_map/rsm,rmac->rsac/dot_general | solution.py:110
  117.9 9.0 %fusion.2 = f32[8,2,8,128,128]{3,4,1,2,0:T(8,128)} fusion(f32[8,8,128,128,1]{3,1,2,0,4:T(8,128)S(1)} %convolution_bitcast_fusion, f32[8,2,128,128]{3,2,1,0:T(8,128)S(1)} %copy-done), kind=kOutput, calls=%fused_computation.9 | convolution fusion | flops 3221225472 | bytes 13631488 | tf_op jit(solution)/shard_map/rpba,rsbc->rpsac/dot_general | solution.py:111
  126.9 9.2 %copy.32 = f32[8,2,8,128,128]{4,0,1,3,2:T(8,128)} copy(f32[8,2,8,128,128]{3,4,1,2,0:T(8,128)} %fusion.2) | data formatting | bytes 16777216 | tf_op jit(solution)/shard_map/rpba,rsbc->rpsac/transpose | solution.py:111
  136.1 7.2 %convolution_bitcast_fusion.1 = f32[4,8,128,128]{3,0,2,1:T(4,128)S(1)} fusion(f32[8,2,8,128,128]{4,0,1,3,2:T(8,128)} %copy.32, s32[8,2]{0,1:T(2,128)S(1)} %get-tuple-element.15), kind=kOutput, calls=%fused_computation.15 | convolution fusion | flops 100663360 | bytes 10485824 | tf_op jit(solution)/shard_map/trp,rpsac->tsac/dot_general | solution.py:116
  143.3 1.0 fusion.32
  144.4 0.4 concatenate.46
  144.8 1.9 %collective-permute-start.13 = (f32[2,10,128,128]{3,0,2,1:T(2,128)S(1)}, f32[2,10,128,128]{3,0,2,1:T(2,128)S(1)}, u32[]{:S(2)}, u32[]{:S(2)}) collective-permute-start(f32[2,10,128,128]{3,0,2,1:T(2,128)S(1)} %concatenate.46), channel_id=1, source_target_pairs={{0,1},{1,2},{2,3},{3,4},{4,5},{5,6},{6,7},{8,9},{9,10},{10,11},{11... | collective-permute-start | bytes 3932168 | tf_op jit(solution)/shard_map/ppermute | solution.py:33
  146.7 17.9 %collective-permute-done.13 = f32[2,10,128,128]{3,0,2,1:T(2,128)S(1)} collective-permute-done((f32[2,10,128,128]{3,0,2,1:T(2,128)S(1)}, f32[2,10,128,128]{3,0,2,1:T(2,128)S(1)}, u32[]{:S(2)}, u32[]{:S(2)}) %collective-permute-start.13) | collective-permute-done | bytes 1310752 | tf_op jit(solution)/shard_map/ppermute | solution.py:33
  164.6 0.6 pad_add_fusion
  165.2 1.2 copy.33
  (5 shorter events, 0.0 us)
Async XLA Ops:
  0.0 89.5 %collective-permute-start.8 = (f32[8,2,128,128]{3,2,1,0:T(8,128)}, f32[8,2,128,128]{3,2,1,0:T(8,128)}, u32[]{:S(2)}, u32[]{:S(2)}) collective-permute-start(f32[8,2,128,128]{3,2,1,0:T(8,128)} %param.8), channel_id=1, source_target_pairs={{0,1},{1,2},{2,3},{3,4},{4,5},{5,6},{6,7},{8,9},{9,10},{10,11},{11... | collective-permute-start | bytes 3145736 | tf_op jit(solution)/shard_map/ppermute | solution.py:18
  1.9 87.6 %collective-permute-start.9 = (f32[8,2,128,128]{3,2,1,0:T(8,128)}, f32[8,2,128,128]{3,2,1,0:T(8,128)}, u32[]{:S(2)}, u32[]{:S(2)}) collective-permute-start(f32[8,2,128,128]{3,2,1,0:T(8,128)} %param.8), channel_id=1, source_target_pairs={{1,0},{2,1},{3,2},{4,3},{5,4},{6,5},{7,6},{9,8},{10,9},{11,10},{12... | collective-permute-start | bytes 3145736 | tf_op jit(solution)/shard_map/ppermute | solution.py:19
  7.2 36.9 %collective-permute-start = (f32[8,2]{0,1:T(2,128)S(1)}, f32[8,2]{0,1:T(2,128)S(1)}, u32[]{:S(2)}, u32[]{:S(2)}) collective-permute-start(f32[8,2]{0,1:T(2,128)S(1)} %get-tuple-element.16), channel_id=1, source_target_pairs={{0,1},{1,2},{2,3},{3,4},{4,5},{5,6},{6,7},{8,9},{9,10},{10,11},{11... | collective-permute-start | bytes 200 | tf_op jit(solution)/shard_map/ppermute | solution.py:18
  9.2 38.4 %collective-permute-start.1 = (f32[8,2]{0,1:T(2,128)S(1)}, f32[8,2]{0,1:T(2,128)S(1)}, u32[]{:S(2)}, u32[]{:S(2)}) collective-permute-start(f32[8,2]{0,1:T(2,128)S(1)} %get-tuple-element.16), channel_id=1, source_target_pairs={{1,0},{2,1},{3,2},{4,3},{5,4},{6,5},{7,6},{9,8},{10,9},{11,10},{12... | collective-permute-start | bytes 200 | tf_op jit(solution)/shard_map/ppermute | solution.py:19
  15.3 6.9 %collective-permute-start.2 = (f32[2]{0:T(128)S(1)}, f32[2]{0:T(128)S(1)}, u32[]{:S(2)}, u32[]{:S(2)}) collective-permute-start(f32[2]{0:T(128)S(1)} %get-tuple-element.20), channel_id=1, source_target_pairs={{24,0},{0,8},{8,16},{16,24},{25,1},{1,9},{9,17},{17,25},{26,2},{2,... | collective-permute-start | bytes 32 | tf_op jit(solution)/shard_map/ppermute | solution.py:27
  22.1 4.5 %collective-permute-start.3 = (f32[2]{0:T(128)S(1)}, f32[2]{0:T(128)S(1)}, u32[]{:S(2)}, u32[]{:S(2)}) collective-permute-start(f32[2]{0:T(128)S(1)} %get-tuple-element.19), channel_id=1, source_target_pairs={{16,0},{24,8},{0,16},{8,24},{17,1},{25,9},{1,17},{9,25},{18,2},{26... | collective-permute-start | bytes 32 | tf_op jit(solution)/shard_map/ppermute | solution.py:27
  26.6 3.5 %collective-permute-start.4 = (f32[2]{0:T(128)S(1)}, f32[2]{0:T(128)S(1)}, u32[]{:S(2)}, u32[]{:S(2)}) collective-permute-start(f32[2]{0:T(128)S(1)} %get-tuple-element.18), channel_id=1, source_target_pairs={{8,0},{16,8},{24,16},{0,24},{9,1},{17,9},{25,17},{1,25},{10,2},{18... | collective-permute-start | bytes 32 | tf_op jit(solution)/shard_map/ppermute | solution.py:27
  30.2 3.6 %collective-permute-start.5 = (f32[2,4]{1,0:T(2,128)S(1)}, f32[2,4]{1,0:T(2,128)S(1)}, u32[]{:S(2)}, u32[]{:S(2)}) collective-permute-start(f32[2,4]{1,0:T(2,128)S(1)} %get-tuple-element.14), channel_id=1, source_target_pairs={{24,0},{0,8},{8,16},{16,24},{25,1},{1,9},{9,17},{17,25},{26,2},{2,... | collective-permute-start | bytes 104 | tf_op jit(solution)/shard_map/ppermute | solution.py:27
  33.8 4.6 %collective-permute-start.6 = (f32[2,4]{1,0:T(2,128)S(1)}, f32[2,4]{1,0:T(2,128)S(1)}, u32[]{:S(2)}, u32[]{:S(2)}) collective-permute-start(f32[2,4]{1,0:T(2,128)S(1)} %get-tuple-element.13), channel_id=1, source_target_pairs={{16,0},{24,8},{0,16},{8,24},{17,1},{25,9},{1,17},{9,25},{18,2},{26... | collective-permute-start | bytes 104 | tf_op jit(solution)/shard_map/ppermute | solution.py:27
  38.3 3.7 %collective-permute-start.7 = (f32[2,4]{1,0:T(2,128)S(1)}, f32[2,4]{1,0:T(2,128)S(1)}, u32[]{:S(2)}, u32[]{:S(2)}) collective-permute-start(f32[2,4]{1,0:T(2,128)S(1)} %get-tuple-element.12), channel_id=1, source_target_pairs={{8,0},{16,8},{24,16},{0,24},{9,1},{17,9},{25,17},{1,25},{10,2},{18... | collective-permute-start | bytes 104 | tf_op jit(solution)/shard_map/ppermute | solution.py:27
  42.0 33.9 %collective-permute-start.10 = (f32[2,4,128,128]{3,2,1,0:T(8,128)}, f32[2,4,128,128]{3,2,1,0:T(8,128)S(1)}, u32[]{:S(2)}, u32[]{:S(2)}) collective-permute-start(f32[2,4,128,128]{3,2,1,0:T(8,128)} %get-tuple-element.10), channel_id=1, source_target_pairs={{24,0},{0,8},{8,16},{16,24},{25,1},{1,9},{9,17},{17,25},{26,2},{2,... | collective-permute-start | bytes 1572872 | tf_op jit(solution)/shard_map/ppermute | solution.py:27
  44.1 37.4 %collective-permute-start.11 = (f32[2,4,128,128]{3,2,1,0:T(8,128)}, f32[2,4,128,128]{3,2,1,0:T(8,128)S(1)}, u32[]{:S(2)}, u32[]{:S(2)}) collective-permute-start(f32[2,4,128,128]{3,2,1,0:T(8,128)} %get-tuple-element.9), channel_id=1, source_target_pairs={{16,0},{24,8},{0,16},{8,24},{17,1},{25,9},{1,17},{9,25},{18,2},{26... | collective-permute-start | bytes 1572872 | tf_op jit(solution)/shard_map/ppermute | solution.py:27
  47.5 37.7 %collective-permute-start.12 = (f32[2,4,128,128]{3,2,1,0:T(8,128)S(1)}, f32[2,4,128,128]{3,2,1,0:T(8,128)S(1)}, u32[]{:S(2)}, u32[]{:S(2)}) collective-permute-start(f32[2,4,128,128]{3,2,1,0:T(8,128)S(1)} %get-tuple-element.8), channel_id=1, source_target_pairs={{8,0},{16,8},{24,16},{0,24},{9,1},{17,9},{25,17},{1,25},{10,2},{18... | collective-permute-start | bytes 1572872 | tf_op jit(solution)/shard_map/ppermute | solution.py:27
  87.0 2.5 %copy-start = (f32[8,2,128,128]{3,2,1,0:T(8,128)S(1)}, f32[8,2,128,128]{3,2,1,0:T(8,128)}, u32[]{:S(2)}) copy-start(f32[8,2,128,128]{3,2,1,0:T(8,128)} %param.8) | copy-start | bytes 3145732
  144.8 19.8 %collective-permute-start.13 = (f32[2,10,128,128]{3,0,2,1:T(2,128)S(1)}, f32[2,10,128,128]{3,0,2,1:T(2,128)S(1)}, u32[]{:S(2)}, u32[]{:S(2)}) collective-permute-start(f32[2,10,128,128]{3,0,2,1:T(2,128)S(1)} %concatenate.46), channel_id=1, source_target_pairs={{0,1},{1,2},{2,3},{3,4},{4,5},{5,6},{6,7},{8,9},{9,10},{10,11},{11... | collective-permute-start | bytes 3932168 | tf_op jit(solution)/shard_map/ppermute | solution.py:33
where the time goes:
time: 167 us; the launch traced here: 166 us
  waiting for transfers between devices  63.8 us (38%)
  starting transfers between devices  32 us (19%)
  matrix products  31.1 us (19%)
  local copies, waits for them, and re-layouts  30.6 us (18%)
  other arithmetic  8.71 us (5%)
    ppermute x9, waiting for transfers between devices, from_behind(): return lax.ppermute(block, axis, route)  45.9 us
    ppermute x1, waiting for transfers between devices, shifted(): lax.ppermute(value, axis, [(source, source + steps) for source in range(l...  17.9 us
    ppermute x9, starting transfers between devices, from_behind(): return lax.ppermute(block, axis, route)  17.2 us
    dot_general x1, matrix products, shards(): jnp.einsum('rkab,rkqbc->rkqac', moved, fetched, precision=lax.Precision.H...  10.5 us
    transpose x1, local copies, waits for them, and re-layouts, shards(): jnp.einsum('rpba,rsbc->rpsac', p_tiles, summed, precision=lax.Precision.H...  9.21 us
    ppermute x2, starting transfers between devices, with_halo(): after = lax.ppermute(leading, axis, down)  9.09 us
    dot_general x1, matrix products, shards(): jnp.einsum('rpba,rsbc->rpsac', p_tiles, summed, precision=lax.Precision.H...  9.05 us
    dot_general x1, matrix products, shards(): jnp.einsum('trp,rpsac->tsac', owner_pick, lifted, precision=lax.Precision...  7.22 us
  transfers between devices with their start and end apart: 14, of which 9 were waited for; matrix products, arithmetic and copies ran while one was open for 8% of the time, Pallas kernels for 0%

commit v1 on v0

v1 whole, which is shorter than its diff:
```python
import functools

import jax
import jax.numpy as jnp
from jax import lax
from jax.experimental import pallas as pl
from jax.experimental.pallas import tpu as pltpu
from jax.sharding import PartitionSpec as P

A_TILES = 4
P_TILES = 2
CAP = 2
SPAN = 6
LANES = 128
ROW_LANE = A_TILES
P_LANE = A_TILES + 1


def split(value):
    high = value.astype(jnp.bfloat16)
    low = (value - high.astype(jnp.float32)).astype(jnp.bfloat16)
    return high, low


def find_row(new_row_of, rows, per_owner, owner, rank):
    seen = jnp.int32(0)
    found = jnp.int32(0)
    for row in range(rows):
        here = lax.div(new_row_of(row), jnp.int32(per_owner)) == owner
        found = jnp.where(here & (seen == rank), row, found)
        seen = seen + here.astype(jnp.int32)
    return found, seen > rank


def kernel(
    span, gx, gy,
    new_row_ref, a_cols_ref, p_cols_ref, a_ref, p_ref,
    own_ref, arrived_ref,
    stage, recv, ext, ext_cat, flipped, products, following,
    table, table_from, table_ext, from_s, ext_s,
    a_send, a_recv, t_send, t_recv, h_send, h_recv, ht_send, ht_recv, n_send, n_recv, local_sem,
):
    rows, tile = p_ref.shape[0], p_ref.shape[2]
    coarse = rows // 4
    chunks = 4 * coarse // 2
    x, y = lax.axis_index("gx"), lax.axis_index("gy")
    device = x * gy + y
    per_owner = rows * gy
    has_left, has_right = y > 0, y < gy - 1

    barrier = pltpu.get_barrier_semaphore()
    for step in range(1, span):
        pl.semaphore_signal(
            barrier, inc=1, device_id={"gx": lax.rem(x + gx - step, gx)},
            device_id_type=pl.DeviceIdType.MESH)

    @pl.when(has_left)
    def _():
        pl.semaphore_signal(
            barrier, inc=1, device_id={"gy": y - 1}, device_id_type=pl.DeviceIdType.MESH)

    @pl.when(has_right)
    def _():
        pl.semaphore_signal(
            barrier, inc=1, device_id={"gy": y + 1}, device_id_type=pl.DeviceIdType.MESH)

    row_id = lax.broadcasted_iota(jnp.int32, (rows, LANES), 0)
    lane_id = lax.broadcasted_iota(jnp.int32, (rows, LANES), 1)
    filled = jnp.zeros((rows, LANES), jnp.int32)
    for row in range(rows):
        entries = [a_cols_ref[row, k] for k in range(A_TILES)]
        entries += [new_row_ref[row]]
        entries += [p_cols_ref[row, q] for q in range(P_TILES)]
        for lane, entry in enumerate(entries):
            filled = jnp.where((row_id == row) & (lane_id == lane), entry, filled)
    table[...] = filled
    table_from[0] = filled
    table_ext[1] = filled

    def put_rows(step, target, slot):
        owner = lax.rem(x + step, gx)
        for rank in range(CAP):
            row, _ = find_row(lambda r: new_row_ref[r], rows, per_owner, owner, rank)
            target[slot, rank] = a_ref[row]

    def a_copy(step):
        return pltpu.make_async_remote_copy(
            stage.at[step], recv.at[step], a_send.at[step], a_recv.at[step],
            device_id={"gx": lax.rem(x + step, gx)}, device_id_type=pl.DeviceIdType.MESH)

    def table_copy(step):
        return pltpu.make_async_remote_copy(
            table, table_from.at[step], t_send.at[step], t_recv.at[step],
            device_id={"gx": lax.rem(x + step, gx)}, device_id_type=pl.DeviceIdType.MESH)

    def halo_copies(side):
        target = y + 1 if side == 0 else y - 1
        place = 0 if side == 0 else 2
        return (
            pltpu.make_async_remote_copy(
                table, table_ext.at[place], ht_send.at[side], ht_recv.at[side],
                device_id={"gy": target}, device_id_type=pl.DeviceIdType.MESH),
            pltpu.make_async_remote_copy(
                p_ref, ext.at[side], h_send.at[side], h_recv.at[side],
                device_id={"gy": target}, device_id_type=pl.DeviceIdType.MESH),
        )

    if gx == 4 and span == 4:
        odd = lax.rem(x, 2)
        send_order = [2, 3 - 2 * odd, 1 + 2 * odd]

        def arrival(n):
            later = n // 2
            return 2 * n * (1 - later) + later * (
                (1 - odd) * (1 + 2 * (n - 2)) + odd * (3 - 2 * (n - 2)))
    else:
        send_order = list(range(1, span))

        def arrival(n):
            return n

    put_rows(send_order[0], stage, send_order[0])
    greeted = span - 1 + jnp.where(has_left, 1, 0) + jnp.where(has_right, 1, 0)
    pl.semaphore_wait(barrier, greeted)
    a_copy(send_order[0]).start()
    for step in range(1, span):
        table_copy(step).start()

    @pl.when(has_right)
    def _():
        for copy in halo_copies(0):
            copy.start()

    @pl.when(has_left)
    def _():
        for copy in halo_copies(1):
            copy.start()

    for step in send_order[1:]:
        put_rows(step, stage, step)
        a_copy(step).start()
    put_rows(0, recv, 0)

    def split_p(source, base):
        def body(row, carry):
            for q in range(P_TILES):
                high, low = split(source[row, q])
                columns = pl.ds(q * tile, tile)
                ext_cat[base + row, pl.ds(0, tile), columns] = high
                ext_cat[base + row, pl.ds(tile, tile), columns] = high
                ext_cat[base + row, pl.ds(2 * tile, tile), columns] = low
            return carry
        lax.fori_loop(0, rows, body, 0)

    def flip(row, carry):
        for q in range(P_TILES):
            flipped[row, q] = p_ref[row, q].T
        return carry

    lax.fori_loop(0, rows, flip, 0)
    split_p(p_ref, rows)

    def clear(n, carry):
        for t in range(coarse):
            own_ref[t, n] = jnp.zeros((tile, tile), jnp.float32)
            following[t, n] = jnp.zeros((tile, tile), jnp.float32)
        return carry

    lax.fori_loop(0, 4 * coarse, clear, 0)

    for step in range(1, span):
        table_copy(step).wait_recv()

    @pl.when(has_left)
    def _():
        for copy in halo_copies(0):
            copy.wait_recv()
        split_p(ext.at[0], 0)

    @pl.when(jnp.logical_not(has_left))
    def _():
        table_ext[0] = jnp.zeros((rows, LANES), jnp.int32)

    @pl.when(has_right)
    def _():
        for copy in halo_copies(1):
            copy.wait_recv()
        split_p(ext.at[1], 2 * rows)

    @pl.when(jnp.logical_not(has_right))
    def _():
        table_ext[2] = jnp.zeros((rows, LANES), jnp.int32)

    to_scalar = (
        pltpu.make_async_copy(table_from, from_s, local_sem.at[0]),
        pltpu.make_async_copy(table_ext, ext_s, local_sem.at[1]),
    )
    for copy in to_scalar:
        copy.start()
    for copy in to_scalar:
        copy.wait()

    def next_copy(n):
        piece = pl.ds(2 * n, 2)
        return pltpu.make_async_remote_copy(
            following.at[:, piece], arrived_ref.at[:, piece], n_send.at[n], n_recv.at[n],
            device_id={"gy": y + 1}, device_id_type=pl.DeviceIdType.MESH)

    def one_distance(n, carry):
        step = arrival(n)

        @pl.when(n > 0)
        def _():
            a_copy(step).wait_recv()

        slots = []
        lifts = [[] for _ in range(2 * coarse)]
        for rank in range(CAP):
            row, there = find_row(
                lambda r: from_s[step, r, ROW_LANE], rows, per_owner, x, rank)
            own_row = lax.rem(from_s[step, row, ROW_LANE], jnp.int32(rows))
            wide = []
            for k in range(A_TILES):
                column = jnp.where(there, from_s[step, row, k] - (device - 1) * rows, rows)
                column = jnp.minimum(jnp.maximum(column, 0), 3 * rows - 1)
                for q in range(P_TILES):
                    goal = ext_s[lax.div(column, rows), lax.rem(column, rows), P_LANE + q]
                    wide.append(jnp.where(there, goal - (device - 1) * coarse, -1))
                high, low = split(recv[step, rank, k])
                left = jnp.concatenate([high, low, high], axis=1)
                products[rank, k] = jnp.dot(
                    left, ext_cat[column], preferred_element_type=jnp.float32)
            slots.append(wide)
            goals = [
                ext_s[1, own_row, P_LANE + p] - device * coarse for p in range(P_TILES)]
            for t in range(2 * coarse):
                lifts[t].append(sum(
                    jnp.where(goals[p] == t, 1.0, 0.0) * flipped[own_row, p]
                    for p in range(P_TILES)))
        lift_cat = []
        for t in range(2 * coarse):
            high, low = split(jnp.concatenate(lifts[t], axis=1))
            lift_cat.append(jnp.concatenate([high, low, high], axis=1))
        lift_cat = jnp.concatenate(lift_cat, axis=0)

        def one_chunk(c, carry):
            halves = []
            for q in range(2):
                w = 2 * c + q
                parts = []
                for rank in range(CAP):
                    total = None
                    for m in range(A_TILES * P_TILES):
                        k, p = m // P_TILES, m % P_TILES
                        weight = jnp.where(slots[rank][m] == w, 1.0, 0.0)
                        term = weight * products[rank, k, :, pl.ds(p * tile, tile)]
                        total = term if total is None else total + term
                    parts.append(total)
                high, low = split(jnp.concatenate(parts, axis=0))
                halves.append(jnp.concatenate([high, high, low], axis=0))
            right = jnp.concatenate(halves, axis=1)
            result = jnp.dot(lift_cat, right, preferred_element_type=jnp.float32)
            for t in range(2 * coarse):
                for q in range(2):
                    value = result[t * tile:(t + 1) * tile, q * tile:(q + 1) * tile]
                    if t < coarse:
                        own_ref[t, 2 * c + q] += value
                    else:
                        following[t - coarse, 2 * c + q] += value

            @pl.when((n == span - 1) & has_right)
            def _():
                next_copy(c).start()

            return carry

        lax.fori_loop(0, chunks, one_chunk, 0)
        return carry

    lax.fori_loop(0, span, one_distance, 0)

    for step in range(1, span):
        table_copy(step).wait_send()
        a_copy(step).wait_send()

    @pl.when(has_right)
    def _():
        for copy in halo_copies(0):
            copy.wait_send()
        for c in range(chunks):
            next_copy(c).wait_send()

    @pl.when(has_left)
    def _():
        for copy in halo_copies(1):
            copy.wait_send()
        for c in range(chunks):
            next_copy(c).wait_recv()


def shards(a_tiles, a_cols, new_row, p_tiles, p_cols):
    rows, tile = a_tiles.shape[0], a_tiles.shape[2]
    gx, gy = lax.axis_size("gx"), lax.axis_size("gy")
    span = min(SPAN, gx)
    coarse = rows // 4
    vmem = pl.BlockSpec(memory_space=pltpu.VMEM)
    smem = pl.BlockSpec(memory_space=pltpu.SMEM)
    band = jax.ShapeDtypeStruct((coarse, 4 * coarse, tile, tile), jnp.float32)
    dma = pltpu.SemaphoreType.DMA
    row_block = (span, CAP, A_TILES, tile, tile)
    own, arrived = pl.pallas_call(
        functools.partial(kernel, span, gx, gy),
        out_shape=(band, band),
        in_specs=[smem, smem, smem, vmem, vmem],
        out_specs=(vmem, pl.BlockSpec(memory_space=pl.ANY)),
        scratch_shapes=[
            pltpu.VMEM(row_block, jnp.float32),
            pltpu.VMEM(row_block, jnp.float32),
            pltpu.VMEM((2, rows, P_TILES, tile, tile), jnp.float32),
            pltpu.VMEM((3 * rows, 3 * tile, P_TILES * tile), jnp.bfloat16),
            pltpu.VMEM((rows, P_TILES, tile, tile), jnp.float32),
            pltpu.VMEM((CAP, A_TILES, tile, P_TILES * tile), jnp.float32),
            pltpu.VMEM((coarse, 4 * coarse, tile, tile), jnp.float32),
            pltpu.VMEM((rows, LANES), jnp.int32),
            pltpu.VMEM((span, rows, LANES), jnp.int32),
            pltpu.VMEM((3, rows, LANES), jnp.int32),
            pltpu.SMEM((span, rows, LANES), jnp.int32),
            pltpu.SMEM((3, rows, LANES), jnp.int32),
            dma((span,)), dma((span,)), dma((span,)), dma((span,)),
            dma((2,)), dma((2,)), dma((2,)), dma((2,)),
            dma((2 * coarse,)), dma((2 * coarse,)), dma((2,)),
        ],
        compiler_params=pltpu.CompilerParams(
            collective_id=0, has_side_effects=True, vmem_limit_bytes=48 * 1024 * 1024),
        name="galerkin",
    )(new_row, a_cols, p_cols, a_tiles, p_tiles)
    arrived = jnp.where(lax.axis_index("gy") > 0, arrived, 0.0)
    pad = ((0, 0), (coarse, 0), (0, 0), (0, 0))
    behind = ((0, 0), (0, coarse), (0, 0), (0, 0))
    return jnp.pad(own, pad) + jnp.pad(arrived, behind)


def solution(mesh):
    in_specs = (
        P(("gx", "gy"), None, None, None),
        P(("gx", "gy"), None),
        P(("gx", "gy")),
        P(("gx", "gy"), None, None, None),
        P(("gx", "gy"), None),
    )
    out_specs = P(("gx", "gy"), None, None, None)
    return jax.shard_map(shards, mesh=mesh, in_specs=in_specs, out_specs=out_specs, check_vma=False)
```

time: 167 us -> 73.5 us (0.44)
  Pallas kernels: 0 us -> 67 us
  waiting for transfers between devices: 63.8 us -> 0 us
  starting transfers between devices: 32 us -> 0 us
  matrix products: 31.1 us -> 0 us
  local copies, waits for them, and re-layouts: 30.6 us -> 4.98 us
  other arithmetic: 8.71 us -> 1.25 us
    pallas_call x0 -> x1, Pallas kernels: none -> 67 us  [shards(): pl.pallas_call(functools.partial(kernel, span, gx, gy), out_shape=(band,...]
    ppermute x14 -> x0, waiting for transfers between devices: 63.8 us -> none  [the longest x9 45.9 us: from_behind(): return lax.ppermute(block, axis, route)]
    ppermute x14 -> x0, starting transfers between devices: 32 us -> none  [the longest x9 17.2 us: from_behind(): return lax.ppermute(block, axis, route)]
    dot_general x4 -> x0, matrix products: 31.1 us -> none  [the longest x1 10.5 us: shards(): jnp.einsum('rkab,rkqbc->rkqac', moved, fetched, precision=lax.Precision.H...]
    transpose x1 -> x0, local copies, waits for them, and re-layouts: 9.21 us -> none  [shards(): jnp.einsum('rpba,rsbc->rpsac', p_tiles, summed, precision=lax.Precision.H...]
    scatter x4 -> x0, local copies, waits for them, and re-layouts: 6.17 us -> none  [the longest x1 2.49 us: shards(): jnp.zeros((span_count * CAP,) + a_tiles.shape[1:], jnp.float32).at[bucket]]
    reshape x1 -> x0, local copies, waits for them, and re-layouts: 5.35 us -> none  [shards(): products.reshape(row_count, A_TILES * P_TILES, tile_size, tile_size)]
    gather x2 -> x0, local copies, waits for them, and re-layouts: 5.21 us -> none  [the longest x1 4.64 us: shards(): fetched = ext_tiles[local_index]]
  transfers between devices with their start and end apart: 14 -> 0, of which waited for: 9 -> 0; matrix products, arithmetic and copies ran while one was open for 8% -> 0% of each run, Pallas kernels for 0% -> 0%
where the time goes in v1:
time: 73.5 us; the launch traced here: 73.2 us
  Pallas kernels  67 us (91%)
  local copies, waits for them, and re-layouts  4.98 us (7%)
  other arithmetic  1.25 us (2%)
    pallas_call x1, Pallas kernels, shards(): pl.pallas_call(functools.partial(kernel, span, gx, gy), out_shape=(band,...  67 us
    unnamed x8, local copies, waits for them, and re-layouts  4.98 us

profile of v1, /device:TPU:12, one launch (start us, length us, event | category | flops | bytes accessed | tf_op | source)
XLA Modules:
  0.0 73.2 jit_solution(10560065177048497930)
XLA Ops:
  0.0 0.8 %copy.6.a_cols_ref = s32[8,4]{1,0:T(8,128)S(1)} copy(s32[8,4]{0,1:T(4,128)} %param.6) | data formatting | bytes 256 | tf_op args[1]
  0.8 0.8 %copy.7.p_cols_ref = s32[8,2]{1,0:T(8,128)S(1)} copy(s32[8,2]{0,1:T(2,128)} %param.9) | data formatting | bytes 128 | tf_op args[4]
  1.5 0.0 copy-start
  1.5 1.6 %copy-done = f32[8,4,128,128]{3,2,1,0:T(8,128)S(1)} copy-done((f32[8,4,128,128]{3,2,1,0:T(8,128)S(1)}, f32[8,4,128,128]{3,2,1,0:T(8,128)}, u32[]{:S(2)}) %copy-start) | copy-done | bytes 2097176
  3.1 0.0 copy-start.1
  3.1 1.2 %copy-done.1 = f32[8,2,128,128]{3,2,1,0:T(8,128)S(1)} copy-done((f32[8,2,128,128]{3,2,1,0:T(8,128)S(1)}, f32[8,2,128,128]{3,2,1,0:T(8,128)}, u32[]{:S(2)}) %copy-start.1) | copy-done | bytes 1048600
  4.3 0.0 copy-start.2
  4.3 0.7 copy-done.2
  5.0 67.0 %galerkin.1 = (f32[2,8,128,128]{3,2,1,0:T(8,128)S(1)}, f32[2,8,128,128]{3,2,1,0:T(8,128)S(1)}) custom-call(s32[8]{0:T(128)S(1)} %copy-done.2, s32[8,4]{1,0:T(8,128)S(1)} %copy.6.a_cols_ref, s32[8,2]{1,0:T(8,128)S(1)} %copy.7.p_cols_ref, f32[8,4,128,128]{3,2,1,0:T(8,128)S(1)} %copy-done, f32[8,2,128,128]{3,2,1,0:T(8,128)S(1)} %copy-done.1), custom_call_target="tpu_custom_call" | custom-call | tf_op jit(solution)/shard_map/galerkin/pallas_call | solution.py:311
  72.0 0.1 broadcast_select_fusion
  72.1 1.2 %pad_add_fusion = f32[2,10,128,128]{3,2,1,0:T(8,128)} fusion(f32[2,8,128,128]{3,2,1,0:T(8,128)S(1)} %broadcast_select_fusion, f32[2,8,128,128]{3,2,1,0:T(8,128)S(1)} %get-tuple-element.7), kind=kLoop, calls=%fused_computation | loop fusion | flops 327680 | bytes 3407872 | tf_op jit(solution)/shard_map/add | solution.py:340
Async XLA Ops:
  1.5 1.6 %copy-start = (f32[8,4,128,128]{3,2,1,0:T(8,128)S(1)}, f32[8,4,128,128]{3,2,1,0:T(8,128)}, u32[]{:S(2)}) copy-start(f32[8,4,128,128]{3,2,1,0:T(8,128)} %a_ref.1) | copy-start | bytes 6291460
  3.1 1.2 %copy-start.1 = (f32[8,2,128,128]{3,2,1,0:T(8,128)S(1)}, f32[8,2,128,128]{3,2,1,0:T(8,128)}, u32[]{:S(2)}) copy-start(f32[8,2,128,128]{3,2,1,0:T(8,128)} %p_ref.1) | copy-start | bytes 3145732
  4.3 0.7 copy-start.2

commit v2 on v1

--- a/solution.py
+++ b/solution.py
@@ -34,11 +34,12 @@
 
 def kernel(
     span, gx, gy,
-    new_row_ref, a_cols_ref, p_cols_ref, a_ref, p_ref,
-    own_ref, arrived_ref,
+    new_row_hbm, a_cols_hbm, p_cols_hbm, a_hbm, p_hbm,
+    own_out, arrived_ref,
+    own_ref, new_row_ref, a_cols_ref, p_cols_ref, a_ref, p_ref,
     stage, recv, ext, ext_cat, flipped, products, following,
     table, table_from, table_ext, from_s, ext_s,
-    a_send, a_recv, t_send, t_recv, h_send, h_recv, ht_send, ht_recv, n_send, n_recv, local_sem,
+    a_send, a_recv, t_send, t_recv, h_send, h_recv, ht_send, ht_recv, n_send, n_recv, local_sem, gate, o_sem,
 ):
     rows, tile = p_ref.shape[0], p_ref.shape[2]
     coarse = rows // 4
@@ -47,6 +48,16 @@
     device = x * gy + y
     per_owner = rows * gy
     has_left, has_right = y > 0, y < gy - 1
+    gated = gx == 4 and span == 4 and gy % 2 == 0
+    first_core = lax.rem(y, 2) == 0
+
+    inputs = [
+        pltpu.make_async_copy(source, target, local_sem.at[n])
+        for n, (source, target) in enumerate((
+            (new_row_hbm, new_row_ref), (a_cols_hbm, a_cols_ref), (p_cols_hbm, p_cols_ref),
+            (a_hbm, a_ref), (p_hbm, p_ref)))]
+    for copy in inputs:
+        copy.start()
 
     barrier = pltpu.get_barrier_semaphore()
     for step in range(1, span):
@@ -64,13 +75,15 @@
         pl.semaphore_signal(
             barrier, inc=1, device_id={"gy": y + 1}, device_id_type=pl.DeviceIdType.MESH)
 
+    for copy in inputs[:3]:
+        copy.wait()
     row_id = lax.broadcasted_iota(jnp.int32, (rows, LANES), 0)
     lane_id = lax.broadcasted_iota(jnp.int32, (rows, LANES), 1)
     filled = jnp.zeros((rows, LANES), jnp.int32)
     for row in range(rows):
-        entries = [a_cols_ref[row, k] for k in range(A_TILES)]
+        entries = [a_cols_ref[k, row] for k in range(A_TILES)]
         entries += [new_row_ref[row]]
-        entries += [p_cols_ref[row, q] for q in range(P_TILES)]
+        entries += [p_cols_ref[q, row] for q in range(P_TILES)]
         for lane, entry in enumerate(entries):
             filled = jnp.where((row_id == row) & (lane_id == lane), entry, filled)
     table[...] = filled
@@ -101,7 +114,7 @@
                 table, table_ext.at[place], ht_send.at[side], ht_recv.at[side],
                 device_id={"gy": target}, device_id_type=pl.DeviceIdType.MESH),
             pltpu.make_async_remote_copy(
-                p_ref, ext.at[side], h_send.at[side], h_recv.at[side],
+                p_hbm, ext.at[side], h_send.at[side], h_recv.at[side],
                 device_id={"gy": target}, device_id_type=pl.DeviceIdType.MESH),
         )
 
@@ -112,13 +125,15 @@
         def arrival(n):
             later = n // 2
             return 2 * n * (1 - later) + later * (
-                (1 - odd) * (1 + 2 * (n - 2)) + odd * (3 - 2 * (n - 2)))
+                (1 - odd) * (3 - 2 * (n - 2)) + odd * (1 + 2 * (n - 2)))
     else:
         send_order = list(range(1, span))
 
         def arrival(n):
             return n
 
+    for copy in inputs[3:]:
+        copy.wait()
     put_rows(send_order[0], stage, send_order[0])
     greeted = span - 1 + jnp.where(has_left, 1, 0) + jnp.where(has_right, 1, 0)
     pl.semaphore_wait(barrier, greeted)
@@ -136,9 +151,14 @@
         for copy in halo_copies(1):
             copy.start()
 
-    for step in send_order[1:]:
+    for n, step in enumerate(send_order[1:]):
         put_rows(step, stage, step)
-        a_copy(step).start()
+        if gated and n == 0:
+            @pl.when(jnp.logical_not(first_core))
+            def _():
+                a_copy(step).start()
+        else:
+            a_copy(step).start()
     put_rows(0, recv, 0)
 
     def split_p(source, base):
@@ -168,6 +188,12 @@
 
     lax.fori_loop(0, 4 * coarse, clear, 0)
 
+    @pl.when(jnp.logical_not(has_left))
+    def _():
+        copy = pltpu.make_async_copy(following, arrived_ref, local_sem.at[0])
+        copy.start()
+        copy.wait()
+
     for step in range(1, span):
         table_copy(step).wait_recv()
 
@@ -206,8 +232,24 @@
             following.at[:, piece], arrived_ref.at[:, piece], n_send.at[n], n_recv.at[n],
             device_id={"gy": y + 1}, device_id_type=pl.DeviceIdType.MESH)
 
+    def own_copy(n):
+        piece = pl.ds(2 * n, 2)
+        return pltpu.make_async_copy(own_ref.at[:, piece], own_out.at[:, piece], o_sem.at[n])
+
     def one_distance(n, carry):
         step = arrival(n)
+        if gated:
+            @pl.when((n == 1) & first_core)
+            def _():
+                pl.semaphore_wait(gate, 1)
+                a_copy(send_order[1]).start()
+
+            @pl.when((n == 1) & jnp.logical_not(first_core))
+            def _():
+                for sent in send_order[:2]:
+                    a_copy(sent).wait_send()
+                pl.semaphore_signal(
+                    gate, inc=1, device_id={"gy": y - 1}, device_id_type=pl.DeviceIdType.MESH)
 
         @pl.when(n > 0)
         def _():
@@ -272,6 +314,10 @@
             def _():
                 next_copy(c).start()
 
+            @pl.when(n == span - 1)
+            def _():
+                own_copy(c).start()
+
             return carry
 
         lax.fori_loop(0, chunks, one_chunk, 0)
@@ -281,7 +327,19 @@
 
     for step in range(1, span):
         table_copy(step).wait_send()
-        a_copy(step).wait_send()
+    if gated:
+        @pl.when(first_core)
+        def _():
+            for step in send_order[:2]:
+                a_copy(step).wait_send()
+
+        a_copy(send_order[2]).wait_send()
+    else:
+        for step in send_order:
+            a_copy(step).wait_send()
+
+    for c in range(chunks):
+        own_copy(c).wait()
 
     @pl.when(has_right)
     def _():
@@ -303,17 +361,21 @@
     gx, gy = lax.axis_size("gx"), lax.axis_size("gy")
     span = min(SPAN, gx)
     coarse = rows // 4
-    vmem = pl.BlockSpec(memory_space=pltpu.VMEM)
-    smem = pl.BlockSpec(memory_space=pltpu.SMEM)
     band = jax.ShapeDtypeStruct((coarse, 4 * coarse, tile, tile), jnp.float32)
     dma = pltpu.SemaphoreType.DMA
     row_block = (span, CAP, A_TILES, tile, tile)
     own, arrived = pl.pallas_call(
         functools.partial(kernel, span, gx, gy),
-        out_shape=(band, band),
-        in_specs=[smem, smem, smem, vmem, vmem],
-        out_specs=(vmem, pl.BlockSpec(memory_space=pl.ANY)),
+        out_shape=[band, band],
+        in_specs=[pl.BlockSpec(memory_space=pl.ANY)] * 5,
+        out_specs=[pl.BlockSpec(memory_space=pl.ANY)] * 2,
         scratch_shapes=[
+            pltpu.VMEM(band.shape, jnp.float32),
+            pltpu.SMEM((rows,), jnp.int32),
+            pltpu.SMEM((A_TILES, rows), jnp.int32),
+            pltpu.SMEM((P_TILES, rows), jnp.int32),
+            pltpu.VMEM(a_tiles.shape, jnp.float32),
+            pltpu.VMEM(p_tiles.shape, jnp.float32),
             pltpu.VMEM(row_block, jnp.float32),
             pltpu.VMEM(row_block, jnp.float32),
             pltpu.VMEM((2, rows, P_TILES, tile, tile), jnp.float32),
@@ -328,13 +390,13 @@
             pltpu.SMEM((3, rows, LANES), jnp.int32),
             dma((span,)), dma((span,)), dma((span,)), dma((span,)),
             dma((2,)), dma((2,)), dma((2,)), dma((2,)),
-            dma((2 * coarse,)), dma((2 * coarse,)), dma((2,)),
+            dma((2 * coarse,)), dma((2 * coarse,)), dma((5,)),
+            pltpu.SemaphoreType.REGULAR, dma((2 * coarse,)),
         ],
         compiler_params=pltpu.CompilerParams(
-            collective_id=0, has_side_effects=True, vmem_limit_bytes=48 * 1024 * 1024),
+            collective_id=0, has_side_effects=True, vmem_limit_bytes=64 * 1024 * 1024),
         name="galerkin",
-    )(new_row, a_cols, p_cols, a_tiles, p_tiles)
-    arrived = jnp.where(lax.axis_index("gy") > 0, arrived, 0.0)
+    )(new_row, a_cols.T, p_cols.T, a_tiles, p_tiles)
     pad = ((0, 0), (coarse, 0), (0, 0), (0, 0))
     behind = ((0, 0), (0, coarse), (0, 0), (0, 0))
     return jnp.pad(own, pad) + jnp.pad(arrived, behind)

time: 73.5 us -> 60.1 us (0.82)
  Pallas kernels: 67 us -> 57 us
  local copies, waits for them, and re-layouts: 4.98 us -> 0 us
  other arithmetic: 1.25 us -> 2.74 us
    pallas_call x1, Pallas kernels: 67 us -> 57 us  [shards(): pl.pallas_call(functools.partial(kernel, span, gx, gy), out_shape=[band,...]
    unnamed x8 -> x0, local copies, waits for them, and re-layouts: 4.98 us -> none
    add x1, other arithmetic: 1.17 us -> 2.74 us  [shards(): return jnp.pad(own, pad) + jnp.pad(arrived, behind)]
where the time goes in v2:
time: 60.1 us; the launch traced here: 59.7 us
  Pallas kernels  57 us (95%)
  other arithmetic  2.74 us (5%)
    pallas_call x1, Pallas kernels, shards(): pl.pallas_call(functools.partial(kernel, span, gx, gy), out_shape=[band,...  57 us
    add x1, other arithmetic, shards(): return jnp.pad(own, pad) + jnp.pad(arrived, behind)  2.74 us

profile of v2, /device:TPU:12, one launch (start us, length us, event | category | flops | bytes accessed | tf_op | source)
XLA Modules:
  0.0 59.7 jit_solution(16639908269056999787)
XLA Ops:
  0.0 57.0 %galerkin.1 = (f32[2,8,128,128]{3,2,1,0:T(8,128)}, f32[2,8,128,128]{3,2,1,0:T(8,128)}) custom-call(s32[8]{0:T(128)} %new_row_hbm.1, s32[4,8]{1,0:T(4,128)} %bitcast.2, s32[2,8]{1,0:T(2,128)} %bitcast.3, f32[8,4,128,128]{3,2,1,0:T(8,128)} %a_hbm.1, f32[8,2,128,128]{3,2,1,0:T(8,128)} %p_hbm.1), custom_call_target="tpu_custom_call" | custom-call | tf_op jit(solution)/shard_map/galerkin/pallas_call | solution.py:367
  57.0 2.7 %pad_add_fusion = f32[2,10,128,128]{3,2,1,0:T(8,128)} fusion(f32[2,8,128,128]{3,2,1,0:T(8,128)} %get-tuple-element.8, f32[2,8,128,128]{3,2,1,0:T(8,128)} %get-tuple-element.7), kind=kLoop, calls=%fused_computation | loop fusion | flops 327680 | bytes 3407872 | tf_op jit(solution)/shard_map/add | solution.py:402

commit v3 on v2

--- a/solution.py
+++ b/solution.py
@@ -35,11 +35,11 @@
 def kernel(
     span, gx, gy,
     new_row_hbm, a_cols_hbm, p_cols_hbm, a_hbm, p_hbm,
-    own_out, arrived_ref,
-    own_ref, new_row_ref, a_cols_ref, p_cols_ref, a_ref, p_ref,
-    stage, recv, ext, ext_cat, flipped, products, following,
+    own_ref, arrived_ref,
+    new_row_ref, a_cols_ref, p_cols_ref, a_ref, p_ref,
+    stage, recv, ext, ext_cat, flipped, products, summed, lifted, following,
     table, table_from, table_ext, from_s, ext_s,
-    a_send, a_recv, t_send, t_recv, h_send, h_recv, ht_send, ht_recv, n_send, n_recv, local_sem, gate, o_sem,
+    a_send, a_recv, t_send, t_recv, h_send, h_recv, ht_send, ht_recv, n_send, n_recv, local_sem, gate,
 ):
     rows, tile = p_ref.shape[0], p_ref.shape[2]
     coarse = rows // 4
@@ -90,15 +90,15 @@
     table_from[0] = filled
     table_ext[1] = filled
 
-    def put_rows(step, target, slot):
+    def put_row(step, rank, target):
         owner = lax.rem(x + step, gx)
-        for rank in range(CAP):
-            row, _ = find_row(lambda r: new_row_ref[r], rows, per_owner, owner, rank)
-            target[slot, rank] = a_ref[row]
-
-    def a_copy(step):
+        row, _ = find_row(lambda r: new_row_ref[r], rows, per_owner, owner, rank)
+        target[step, rank] = a_ref[row]
+
+    def a_copy(step, rank):
         return pltpu.make_async_remote_copy(
-            stage.at[step], recv.at[step], a_send.at[step], a_recv.at[step],
+            stage.at[step, rank], recv.at[step, rank],
+            a_send.at[step, rank], a_recv.at[step, rank],
             device_id={"gx": lax.rem(x + step, gx)}, device_id_type=pl.DeviceIdType.MESH)
 
     def table_copy(step):
@@ -134,10 +134,12 @@
 
     for copy in inputs[3:]:
         copy.wait()
-    put_rows(send_order[0], stage, send_order[0])
+    put_row(send_order[0], 0, stage)
     greeted = span - 1 + jnp.where(has_left, 1, 0) + jnp.where(has_right, 1, 0)
     pl.semaphore_wait(barrier, greeted)
-    a_copy(send_order[0]).start()
+    a_copy(send_order[0], 0).start()
+    put_row(send_order[0], 1, stage)
+    a_copy(send_order[0], 1).start()
     for step in range(1, span):
         table_copy(step).start()
 
@@ -151,15 +153,14 @@
         for copy in halo_copies(1):
             copy.start()
 
-    for n, step in enumerate(send_order[1:]):
-        put_rows(step, stage, step)
-        if gated and n == 0:
-            @pl.when(jnp.logical_not(first_core))
-            def _():
-                a_copy(step).start()
-        else:
-            a_copy(step).start()
-    put_rows(0, recv, 0)
+    held = send_order[1] if gated else None
+    for step in reversed(send_order[1:]):
+        for rank in range(CAP):
+            put_row(step, rank, stage)
+            if step is not held:
+                a_copy(step, rank).start()
+    for rank in range(CAP):
+        put_row(0, rank, recv)
 
     def split_p(source, base):
         def body(row, carry):
@@ -232,114 +233,123 @@
             following.at[:, piece], arrived_ref.at[:, piece], n_send.at[n], n_recv.at[n],
             device_id={"gy": y + 1}, device_id_type=pl.DeviceIdType.MESH)
 
-    def own_copy(n):
-        piece = pl.ds(2 * n, 2)
-        return pltpu.make_async_copy(own_ref.at[:, piece], own_out.at[:, piece], o_sem.at[n])
+    def flow(n):
+        def hand_on(rank):
+            pl.semaphore_signal(
+                gate.at[rank], inc=1, device_id={"gy": y - 1},
+                device_id_type=pl.DeviceIdType.MESH)
+
+        @pl.when((n == 1) & jnp.logical_not(first_core))
+        def _():
+            for rank in range(CAP):
+                a_copy(send_order[0], rank).wait_send()
+                a_copy(held, rank).start()
+
+        @pl.when((n == span - 1) & jnp.logical_not(first_core))
+        def _():
+            for rank in range(CAP):
+                a_copy(held, rank).wait_send()
+                hand_on(rank)
+
+        @pl.when((n == span - 1) & first_core)
+        def _():
+            for rank in range(CAP):
+                pl.semaphore_wait(gate.at[rank], 1)
+                a_copy(held, rank).start()
 
     def one_distance(n, carry):
         step = arrival(n)
         if gated:
-            @pl.when((n == 1) & first_core)
-            def _():
-                pl.semaphore_wait(gate, 1)
-                a_copy(send_order[1]).start()
-
-            @pl.when((n == 1) & jnp.logical_not(first_core))
-            def _():
-                for sent in send_order[:2]:
-                    a_copy(sent).wait_send()
-                pl.semaphore_signal(
-                    gate, inc=1, device_id={"gy": y - 1}, device_id_type=pl.DeviceIdType.MESH)
-
-        @pl.when(n > 0)
-        def _():
-            a_copy(step).wait_recv()
-
-        slots = []
+            flow(n)
+
         lifts = [[] for _ in range(2 * coarse)]
         for rank in range(CAP):
             row, there = find_row(
                 lambda r: from_s[step, r, ROW_LANE], rows, per_owner, x, rank)
             own_row = lax.rem(from_s[step, row, ROW_LANE], jnp.int32(rows))
-            wide = []
-            for k in range(A_TILES):
-                column = jnp.where(there, from_s[step, row, k] - (device - 1) * rows, rows)
-                column = jnp.minimum(jnp.maximum(column, 0), 3 * rows - 1)
-                for q in range(P_TILES):
-                    goal = ext_s[lax.div(column, rows), lax.rem(column, rows), P_LANE + q]
-                    wide.append(jnp.where(there, goal - (device - 1) * coarse, -1))
-                high, low = split(recv[step, rank, k])
-                left = jnp.concatenate([high, low, high], axis=1)
-                products[rank, k] = jnp.dot(
-                    left, ext_cat[column], preferred_element_type=jnp.float32)
-            slots.append(wide)
             goals = [
                 ext_s[1, own_row, P_LANE + p] - device * coarse for p in range(P_TILES)]
             for t in range(2 * coarse):
                 lifts[t].append(sum(
                     jnp.where(goals[p] == t, 1.0, 0.0) * flipped[own_row, p]
                     for p in range(P_TILES)))
-        lift_cat = []
-        for t in range(2 * coarse):
-            high, low = split(jnp.concatenate(lifts[t], axis=1))
-            lift_cat.append(jnp.concatenate([high, low, high], axis=1))
-        lift_cat = jnp.concatenate(lift_cat, axis=0)
-
-        def one_chunk(c, carry):
-            halves = []
-            for q in range(2):
-                w = 2 * c + q
-                parts = []
-                for rank in range(CAP):
+            wide, columns = [], []
+            for k in range(A_TILES):
+                column = jnp.where(there, from_s[step, row, k] - (device - 1) * rows, rows)
+                column = jnp.minimum(jnp.maximum(column, 0), 3 * rows - 1)
+                columns.append(column)
+                for q in range(P_TILES):
+                    goal = ext_s[lax.div(column, rows), lax.rem(column, rows), P_LANE + q]
+                    wide.append(jnp.where(there, goal - (device - 1) * coarse, -1))
+
+            @pl.when(n > 0)
+            def _():
+                a_copy(step, rank).wait_recv()
+
+            for k in range(A_TILES):
+                high, low = split(recv[step, rank, k])
+                left = jnp.concatenate([high, low, high], axis=1)
+                products[k] = jnp.dot(
+                    left, ext_cat[columns[k]], preferred_element_type=jnp.float32)
+
+            def gather(c, carry):
+                for q in range(2):
                     total = None
                     for m in range(A_TILES * P_TILES):
                         k, p = m // P_TILES, m % P_TILES
-                        weight = jnp.where(slots[rank][m] == w, 1.0, 0.0)
-                        term = weight * products[rank, k, :, pl.ds(p * tile, tile)]
+                        weight = jnp.where(wide[m] == 2 * c + q, 1.0, 0.0)
+                        term = weight * products[k, :, pl.ds(p * tile, tile)]
                         total = term if total is None else total + term
-                    parts.append(total)
-                high, low = split(jnp.concatenate(parts, axis=0))
-                halves.append(jnp.concatenate([high, high, low], axis=0))
-            right = jnp.concatenate(halves, axis=1)
-            result = jnp.dot(lift_cat, right, preferred_element_type=jnp.float32)
-            for t in range(2 * coarse):
+                    high, low = split(total)
+                    here = pl.ds(q * tile, tile)
+                    for part, value in enumerate((high, high, low)):
+                        summed[c, pl.ds((part * CAP + rank) * tile, tile), here] = value
+                return carry
+
+            lax.fori_loop(0, chunks, gather, 0)
+
+        for t in range(2 * coarse):
+            high, low = split(jnp.concatenate(lifts[t], axis=1))
+            lifted[pl.ds(t * tile, tile)] = jnp.concatenate([high, low, high], axis=1)
+
+        def one_chunk(c, first, target):
+            result = jnp.dot(
+                lifted[pl.ds(first * tile, coarse * tile)], summed[c],
+                preferred_element_type=jnp.float32)
+            for t in range(coarse):
                 for q in range(2):
-                    value = result[t * tile:(t + 1) * tile, q * tile:(q + 1) * tile]
-                    if t < coarse:
-                        own_ref[t, 2 * c + q] += value
-                    else:
-                        following[t - coarse, 2 * c + q] += value
+                    target[t, 2 * c + q] += (
+                        result[t * tile:(t + 1) * tile, q * tile:(q + 1) * tile])
+
+        def next_chunk(c, carry):
+            one_chunk(c, coarse, following)
 
             @pl.when((n == span - 1) & has_right)
             def _():
                 next_copy(c).start()
 
-            @pl.when(n == span - 1)
-            def _():
-                own_copy(c).start()
-
             return carry
 
-        lax.fori_loop(0, chunks, one_chunk, 0)
+        def own_chunk(c, carry):
+            one_chunk(c, 0, own_ref)
+            return carry
+
+        lax.fori_loop(0, chunks, next_chunk, 0)
+        lax.fori_loop(0, chunks, own_chunk, 0)
         return carry
 
     lax.fori_loop(0, span, one_distance, 0)
 
     for step in range(1, span):
         table_copy(step).wait_send()
-    if gated:
-        @pl.when(first_core)
-        def _():
-            for step in send_order[:2]:
-                a_copy(step).wait_send()
-
-        a_copy(send_order[2]).wait_send()
-    else:
-        for step in send_order:
-            a_copy(step).wait_send()
-
-    for c in range(chunks):
-        own_copy(c).wait()
+    for step in send_order:
+        for rank in range(CAP):
+            if gated and step is not send_order[2]:
+                @pl.when(first_core)
+                def _():
+                    a_copy(step, rank).wait_send()
+            else:
+                a_copy(step, rank).wait_send()
 
     @pl.when(has_right)
     def _():
@@ -362,15 +372,18 @@
     span = min(SPAN, gx)
     coarse = rows // 4
     band = jax.ShapeDtypeStruct((coarse, 4 * coarse, tile, tile), jnp.float32)
+    band_in = pltpu.VMEM(band.shape, jnp.float32)
     dma = pltpu.SemaphoreType.DMA
     row_block = (span, CAP, A_TILES, tile, tile)
+    operands = [
+        pltpu.with_memory_space_constraint(value, pltpu.HBM)
+        for value in (new_row, a_cols.T, p_cols.T, a_tiles, p_tiles)]
     own, arrived = pl.pallas_call(
         functools.partial(kernel, span, gx, gy),
-        out_shape=[band, band],
+        out_shape=[band_in, band_in],
         in_specs=[pl.BlockSpec(memory_space=pl.ANY)] * 5,
-        out_specs=[pl.BlockSpec(memory_space=pl.ANY)] * 2,
+        out_specs=[pl.BlockSpec(memory_space=pltpu.VMEM)] * 2,
         scratch_shapes=[
-            pltpu.VMEM(band.shape, jnp.float32),
             pltpu.SMEM((rows,), jnp.int32),
             pltpu.SMEM((A_TILES, rows), jnp.int32),
             pltpu.SMEM((P_TILES, rows), jnp.int32),
@@ -381,22 +394,24 @@
             pltpu.VMEM((2, rows, P_TILES, tile, tile), jnp.float32),
             pltpu.VMEM((3 * rows, 3 * tile, P_TILES * tile), jnp.bfloat16),
             pltpu.VMEM((rows, P_TILES, tile, tile), jnp.float32),
-            pltpu.VMEM((CAP, A_TILES, tile, P_TILES * tile), jnp.float32),
+            pltpu.VMEM((A_TILES, tile, P_TILES * tile), jnp.float32),
+            pltpu.VMEM((2 * coarse, 3 * CAP * tile, 2 * tile), jnp.bfloat16),
+            pltpu.VMEM((2 * coarse * tile, 3 * CAP * tile), jnp.bfloat16),
             pltpu.VMEM((coarse, 4 * coarse, tile, tile), jnp.float32),
             pltpu.VMEM((rows, LANES), jnp.int32),
             pltpu.VMEM((span, rows, LANES), jnp.int32),
             pltpu.VMEM((3, rows, LANES), jnp.int32),
             pltpu.SMEM((span, rows, LANES), jnp.int32),
             pltpu.SMEM((3, rows, LANES), jnp.int32),
-            dma((span,)), dma((span,)), dma((span,)), dma((span,)),
+            dma((span, CAP)), dma((span, CAP)), dma((span,)), dma((span,)),
             dma((2,)), dma((2,)), dma((2,)), dma((2,)),
             dma((2 * coarse,)), dma((2 * coarse,)), dma((5,)),
-            pltpu.SemaphoreType.REGULAR, dma((2 * coarse,)),
+            pltpu.SemaphoreType.REGULAR((CAP,)),
         ],
         compiler_params=pltpu.CompilerParams(
-            collective_id=0, has_side_effects=True, vmem_limit_bytes=64 * 1024 * 1024),
+            collective_id=0, has_side_effects=True, vmem_limit_bytes=48 * 1024 * 1024),
         name="galerkin",
-    )(new_row, a_cols.T, p_cols.T, a_tiles, p_tiles)
+    )(*operands)
     pad = ((0, 0), (coarse, 0), (0, 0), (0, 0))
     behind = ((0, 0), (0, coarse), (0, 0), (0, 0))
     return jnp.pad(own, pad) + jnp.pad(arrived, behind)

time: 60.1 us -> 69.1 us (1.15)
  Pallas kernels: 57 us -> 67.8 us
  other arithmetic: 2.74 us -> 1.2 us
    pallas_call x1, Pallas kernels: 57 us -> 67.8 us  [shards(): pl.pallas_call(functools.partial(kernel, span, gx, gy), out_shape=[band_i...]
    add x1, other arithmetic: 2.74 us -> 1.2 us  [shards(): return jnp.pad(own, pad) + jnp.pad(arrived, behind)]
where the time goes in v3:
time: 69.1 us; the launch traced here: 69 us
  Pallas kernels  67.8 us (98%)
  other arithmetic  1.2 us (2%)
    pallas_call x1, Pallas kernels, shards(): pl.pallas_call(functools.partial(kernel, span, gx, gy), out_shape=[band_i...  67.8 us

profile of v3, /device:TPU:12, one launch (start us, length us, event | category | flops | bytes accessed | tf_op | source)
XLA Modules:
  0.0 69.0 jit_solution(17104806936722430711)
XLA Ops:
  0.0 67.8 %galerkin.1 = (f32[2,8,128,128]{3,2,1,0:T(8,128)S(1)}, f32[2,8,128,128]{3,2,1,0:T(8,128)S(1)}) custom-call(s32[8]{0:T(128)} %new_row_hbm.1, s32[4,8]{1,0:T(4,128)} %bitcast.2, s32[2,8]{1,0:T(2,128)} %bitcast.3, f32[8,4,128,128]{3,2,1,0:T(8,128)} %a_hbm.1, f32[8,2,128,128]{3,2,1,0:T(8,128)} %p_hbm.1), custom_call_target="tpu_custom_call" | custom-call | tf_op jit(solution)/shard_map/galerkin/pallas_call | solution.py:381
  67.8 1.2 %pad_add_fusion = f32[2,10,128,128]{3,2,1,0:T(8,128)} fusion(f32[2,8,128,128]{3,2,1,0:T(8,128)S(1)} %get-tuple-element.8, f32[2,8,128,128]{3,2,1,0:T(8,128)S(1)} %get-tuple-element.7), kind=kLoop, calls=%fused_computation | loop fusion | flops 327680 | bytes 3407872 | tf_op jit(solution)/shard_map/add | solution.py:417

commit v4 on v3

--- a/solution.py
+++ b/solution.py
@@ -154,10 +154,14 @@
             copy.start()
 
     held = send_order[1] if gated else None
-    for step in reversed(send_order[1:]):
+    for step in send_order[1:]:
         for rank in range(CAP):
             put_row(step, rank, stage)
-            if step is not held:
+            if step is held:
+                @pl.when(jnp.logical_not(first_core))
+                def _():
+                    a_copy(step, rank).start()
+            else:
                 a_copy(step, rank).start()
     for rank in range(CAP):
         put_row(0, rank, recv)
@@ -243,15 +247,11 @@
         def _():
             for rank in range(CAP):
                 a_copy(send_order[0], rank).wait_send()
-                a_copy(held, rank).start()
-
-        @pl.when((n == span - 1) & jnp.logical_not(first_core))
-        def _():
             for rank in range(CAP):
                 a_copy(held, rank).wait_send()
                 hand_on(rank)
 
-        @pl.when((n == span - 1) & first_core)
+        @pl.when((n == 1) & first_core)
         def _():
             for rank in range(CAP):
                 pl.semaphore_wait(gate.at[rank], 1)

time: 69.1 us -> 62.8 us (0.909)
  the two profiles are of different devices: /device:TPU:12 before, /device:TPU:4 now
where the time goes in v4:
time: 62.8 us; the launch traced here: 62.7 us
  Pallas kernels  61.5 us (98%)
  other arithmetic  1.2 us (2%)
    pallas_call x1, Pallas kernels, shards(): pl.pallas_call(functools.partial(kernel, span, gx, gy), out_shape=[band_i...  61.5 us

profile of v4, /device:TPU:4, one launch (start us, length us, event | category | flops | bytes accessed | tf_op | source)
XLA Modules:
  0.0 62.7 jit_solution(15862858673514252356)
XLA Ops:
  0.0 61.5 %galerkin.1 = (f32[2,8,128,128]{3,2,1,0:T(8,128)S(1)}, f32[2,8,128,128]{3,2,1,0:T(8,128)S(1)}) custom-call(s32[8]{0:T(128)} %new_row_hbm.1, s32[4,8]{1,0:T(4,128)} %bitcast.2, s32[2,8]{1,0:T(2,128)} %bitcast.3, f32[8,4,128,128]{3,2,1,0:T(8,128)} %a_hbm.1, f32[8,2,128,128]{3,2,1,0:T(8,128)} %p_hbm.1), custom_call_target="tpu_custom_call" | custom-call | tf_op jit(solution)/shard_map/galerkin/pallas_call | solution.py:381
  61.5 1.2 %pad_add_fusion = f32[2,10,128,128]{3,2,1,0:T(8,128)} fusion(f32[2,8,128,128]{3,2,1,0:T(8,128)S(1)} %get-tuple-element.8, f32[2,8,128,128]{3,2,1,0:T(8,128)S(1)} %get-tuple-element.7), kind=kLoop, calls=%fused_computation | loop fusion | flops 327680 | bytes 3407872 | tf_op jit(solution)/shard_map/add | solution.py:417

commit v5 on v4

--- a/solution.py
+++ b/solution.py
@@ -37,7 +37,7 @@
     new_row_hbm, a_cols_hbm, p_cols_hbm, a_hbm, p_hbm,
     own_ref, arrived_ref,
     new_row_ref, a_cols_ref, p_cols_ref, a_ref, p_ref,
-    stage, recv, ext, ext_cat, flipped, products, summed, lifted, following,
+    stage, recv, ext, ext_cat, flipped, products, following,
     table, table_from, table_ext, from_s, ext_s,
     a_send, a_recv, t_send, t_recv, h_send, h_recv, ht_send, ht_recv, n_send, n_recv, local_sem, gate,
 ):
@@ -123,9 +123,7 @@
         send_order = [2, 3 - 2 * odd, 1 + 2 * odd]
 
         def arrival(n):
-            later = n // 2
-            return 2 * n * (1 - later) + later * (
-                (1 - odd) * (3 - 2 * (n - 2)) + odd * (1 + 2 * (n - 2)))
+            return lax.rem(4 + (2 * odd - 1) * n, 4)
     else:
         send_order = list(range(1, span))
 
@@ -137,9 +135,17 @@
     put_row(send_order[0], 0, stage)
     greeted = span - 1 + jnp.where(has_left, 1, 0) + jnp.where(has_right, 1, 0)
     pl.semaphore_wait(barrier, greeted)
-    a_copy(send_order[0], 0).start()
+    def send_row(step, rank):
+        if gated and step is not send_order[2]:
+            @pl.when(jnp.logical_not(first_core))
+            def _():
+                a_copy(step, rank).start()
+        else:
+            a_copy(step, rank).start()
+
+    send_row(send_order[0], 0)
     put_row(send_order[0], 1, stage)
-    a_copy(send_order[0], 1).start()
+    send_row(send_order[0], 1)
     for step in range(1, span):
         table_copy(step).start()
 
@@ -153,16 +159,10 @@
         for copy in halo_copies(1):
             copy.start()
 
-    held = send_order[1] if gated else None
     for step in send_order[1:]:
         for rank in range(CAP):
             put_row(step, rank, stage)
-            if step is held:
-                @pl.when(jnp.logical_not(first_core))
-                def _():
-                    a_copy(step, rank).start()
-            else:
-                a_copy(step, rank).start()
+            send_row(step, rank)
     for rank in range(CAP):
         put_row(0, rank, recv)
 
@@ -238,30 +238,28 @@
             device_id={"gy": y + 1}, device_id_type=pl.DeviceIdType.MESH)
 
     def flow(n):
-        def hand_on(rank):
-            pl.semaphore_signal(
-                gate.at[rank], inc=1, device_id={"gy": y - 1},
-                device_id_type=pl.DeviceIdType.MESH)
-
         @pl.when((n == 1) & jnp.logical_not(first_core))
         def _():
-            for rank in range(CAP):
-                a_copy(send_order[0], rank).wait_send()
-            for rank in range(CAP):
-                a_copy(held, rank).wait_send()
-                hand_on(rank)
+            for pair, step in enumerate(send_order[:2]):
+                for rank in range(CAP):
+                    a_copy(step, rank).wait_send()
+                pl.semaphore_signal(
+                    gate.at[pair], inc=1, device_id={"gy": y - 1},
+                    device_id_type=pl.DeviceIdType.MESH)
 
         @pl.when((n == 1) & first_core)
         def _():
-            for rank in range(CAP):
-                pl.semaphore_wait(gate.at[rank], 1)
-                a_copy(held, rank).start()
+            for pair, step in enumerate(send_order[:2]):
+                pl.semaphore_wait(gate.at[pair], 1)
+                for rank in range(CAP):
+                    a_copy(step, rank).start()
 
     def one_distance(n, carry):
         step = arrival(n)
         if gated:
             flow(n)
 
+        slots = []
         lifts = [[] for _ in range(2 * coarse)]
         for rank in range(CAP):
             row, there = find_row(
@@ -286,43 +284,43 @@
             def _():
                 a_copy(step, rank).wait_recv()
 
+            slots.append(wide)
             for k in range(A_TILES):
                 high, low = split(recv[step, rank, k])
                 left = jnp.concatenate([high, low, high], axis=1)
-                products[k] = jnp.dot(
+                products[rank, k] = jnp.dot(
                     left, ext_cat[columns[k]], preferred_element_type=jnp.float32)
 
-            def gather(c, carry):
-                for q in range(2):
+        lift_cat = []
+        for t in range(2 * coarse):
+            high, low = split(jnp.concatenate(lifts[t], axis=1))
+            lift_cat.append(jnp.concatenate([high, low, high], axis=1))
+        lift_cat = jnp.concatenate(lift_cat, axis=0)
+
+        def one_chunk(c, carry):
+            halves = []
+            for q in range(2):
+                w = 2 * c + q
+                parts = []
+                for rank in range(CAP):
                     total = None
                     for m in range(A_TILES * P_TILES):
                         k, p = m // P_TILES, m % P_TILES
-                        weight = jnp.where(wide[m] == 2 * c + q, 1.0, 0.0)
-                        term = weight * products[k, :, pl.ds(p * tile, tile)]
+                        weight = jnp.where(slots[rank][m] == w, 1.0, 0.0)
+                        term = weight * products[rank, k, :, pl.ds(p * tile, tile)]
                         total = term if total is None else total + term
-                    high, low = split(total)
-                    here = pl.ds(q * tile, tile)
-                    for part, value in enumerate((high, high, low)):
-                        summed[c, pl.ds((part * CAP + rank) * tile, tile), here] = value
-                return carry
-
-            lax.fori_loop(0, chunks, gather, 0)
-
-        for t in range(2 * coarse):
-            high, low = split(jnp.concatenate(lifts[t], axis=1))
-            lifted[pl.ds(t * tile, tile)] = jnp.concatenate([high, low, high], axis=1)
-
-        def one_chunk(c, first, target):
-            result = jnp.dot(
-                lifted[pl.ds(first * tile, coarse * tile)], summed[c],
-                preferred_element_type=jnp.float32)
-            for t in range(coarse):
+                    parts.append(total)
+                high, low = split(jnp.concatenate(parts, axis=0))
+                halves.append(jnp.concatenate([high, high, low], axis=0))
+            right = jnp.concatenate(halves, axis=1)
+            result = jnp.dot(lift_cat, right, preferred_element_type=jnp.float32)
+            for t in range(2 * coarse):
                 for q in range(2):
-                    target[t, 2 * c + q] += (
-                        result[t * tile:(t + 1) * tile, q * tile:(q + 1) * tile])
-
-        def next_chunk(c, carry):
-            one_chunk(c, coarse, following)
+                    value = result[t * tile:(t + 1) * tile, q * tile:(q + 1) * tile]
+                    if t < coarse:
+                        own_ref[t, 2 * c + q] += value
+                    else:
+                        following[t - coarse, 2 * c + q] += value
 
             @pl.when((n == span - 1) & has_right)
             def _():
@@ -330,12 +328,7 @@
 
             return carry
 
-        def own_chunk(c, carry):
-            one_chunk(c, 0, own_ref)
-            return carry
-
-        lax.fori_loop(0, chunks, next_chunk, 0)
-        lax.fori_loop(0, chunks, own_chunk, 0)
+        lax.fori_loop(0, chunks, one_chunk, 0)
         return carry
 
     lax.fori_loop(0, span, one_distance, 0)
@@ -394,9 +387,7 @@
             pltpu.VMEM((2, rows, P_TILES, tile, tile), jnp.float32),
             pltpu.VMEM((3 * rows, 3 * tile, P_TILES * tile), jnp.bfloat16),
             pltpu.VMEM((rows, P_TILES, tile, tile), jnp.float32),
-            pltpu.VMEM((A_TILES, tile, P_TILES * tile), jnp.float32),
-            pltpu.VMEM((2 * coarse, 3 * CAP * tile, 2 * tile), jnp.bfloat16),
-            pltpu.VMEM((2 * coarse * tile, 3 * CAP * tile), jnp.bfloat16),
+            pltpu.VMEM((CAP, A_TILES, tile, P_TILES * tile), jnp.float32),
             pltpu.VMEM((coarse, 4 * coarse, tile, tile), jnp.float32),
             pltpu.VMEM((rows, LANES), jnp.int32),
             pltpu.VMEM((span, rows, LANES), jnp.int32),
@@ -406,7 +397,7 @@
             dma((span, CAP)), dma((span, CAP)), dma((span,)), dma((span,)),
             dma((2,)), dma((2,)), dma((2,)), dma((2,)),
             dma((2 * coarse,)), dma((2 * coarse,)), dma((5,)),
-            pltpu.SemaphoreType.REGULAR((CAP,)),
+            pltpu.SemaphoreType.REGULAR((2,)),
         ],
         compiler_params=pltpu.CompilerParams(
             collective_id=0, has_side_effects=True, vmem_limit_bytes=48 * 1024 * 1024),

time: 62.8 us -> 61.9 us (0.986)
  the two profiles are of different devices: /device:TPU:4 before, /device:TPU:12 now
where the time goes in v5:
time: 61.9 us; the launch traced here: 60.8 us
  Pallas kernels  59.6 us (96%)
  other arithmetic  1.2 us (2%)
    pallas_call x1, Pallas kernels, shards(): pl.pallas_call(functools.partial(kernel, span, gx, gy), out_shape=[band_i...  59.6 us

profile of v5, /device:TPU:12, one launch (start us, length us, event | category | flops | bytes accessed | tf_op | source)
XLA Modules:
  0.0 60.8 jit_solution(6822055996064441240)
XLA Ops:
  0.0 59.6 %galerkin.1 = (f32[2,8,128,128]{3,2,1,0:T(8,128)S(1)}, f32[2,8,128,128]{3,2,1,0:T(8,128)S(1)}) custom-call(s32[8]{0:T(128)} %new_row_hbm.1, s32[4,8]{1,0:T(4,128)} %bitcast.2, s32[2,8]{1,0:T(2,128)} %bitcast.3, f32[8,4,128,128]{3,2,1,0:T(8,128)} %a_hbm.1, f32[8,2,128,128]{3,2,1,0:T(8,128)} %p_hbm.1), custom_call_target="tpu_custom_call" | custom-call | tf_op jit(solution)/shard_map/galerkin/pallas_call | solution.py:374
  59.6 1.2 %pad_add_fusion = f32[2,10,128,128]{3,2,1,0:T(8,128)} fusion(f32[2,8,128,128]{3,2,1,0:T(8,128)S(1)} %get-tuple-element.8, f32[2,8,128,128]{3,2,1,0:T(8,128)S(1)} %get-tuple-element.7), kind=kLoop, calls=%fused_computation | loop fusion | flops 327680 | bytes 3407872 | tf_op jit(solution)/shard_map/add | solution.py:408

commit v6 on v5

--- a/solution.py
+++ b/solution.py
@@ -32,6 +32,13 @@
     return found, seen > rank
 
 
+def may_reach(k, p, place):
+    columns = (1,) if k == 0 else (0, 1, 2)
+    if p == 0:
+        return place in columns
+    return place - 1 in columns or place == 1
+
+
 def kernel(
     span, gx, gy,
     new_row_hbm, a_cols_hbm, p_cols_hbm, a_hbm, p_hbm,
@@ -39,7 +46,7 @@
     new_row_ref, a_cols_ref, p_cols_ref, a_ref, p_ref,
     stage, recv, ext, ext_cat, flipped, products, following,
     table, table_from, table_ext, from_s, ext_s,
-    a_send, a_recv, t_send, t_recv, h_send, h_recv, ht_send, ht_recv, n_send, n_recv, local_sem, gate,
+    a_send, a_recv, t_send, t_recv, h_send, h_recv, ht_send, ht_recv, n_send, n_recv, local_sem,
 ):
     rows, tile = p_ref.shape[0], p_ref.shape[2]
     coarse = rows // 4
@@ -48,7 +55,7 @@
     device = x * gy + y
     per_owner = rows * gy
     has_left, has_right = y > 0, y < gy - 1
-    gated = gx == 4 and span == 4 and gy % 2 == 0
+    paced = gx == 4 and span == 4 and gy % 2 == 0
     first_core = lax.rem(y, 2) == 0
 
     inputs = [
@@ -123,7 +130,9 @@
         send_order = [2, 3 - 2 * odd, 1 + 2 * odd]
 
         def arrival(n):
-            return lax.rem(4 + (2 * odd - 1) * n, 4)
+            later = n // 2
+            return 2 * n * (1 - later) + later * (
+                (1 - odd) * (3 - 2 * (n - 2)) + odd * (1 + 2 * (n - 2)))
     else:
         send_order = list(range(1, span))
 
@@ -136,7 +145,7 @@
     greeted = span - 1 + jnp.where(has_left, 1, 0) + jnp.where(has_right, 1, 0)
     pl.semaphore_wait(barrier, greeted)
     def send_row(step, rank):
-        if gated and step is not send_order[2]:
+        if paced and step is send_order[1]:
             @pl.when(jnp.logical_not(first_core))
             def _():
                 a_copy(step, rank).start()
@@ -237,27 +246,14 @@
             following.at[:, piece], arrived_ref.at[:, piece], n_send.at[n], n_recv.at[n],
             device_id={"gy": y + 1}, device_id_type=pl.DeviceIdType.MESH)
 
-    def flow(n):
-        @pl.when((n == 1) & jnp.logical_not(first_core))
-        def _():
-            for pair, step in enumerate(send_order[:2]):
-                for rank in range(CAP):
-                    a_copy(step, rank).wait_send()
-                pl.semaphore_signal(
-                    gate.at[pair], inc=1, device_id={"gy": y - 1},
-                    device_id_type=pl.DeviceIdType.MESH)
-
-        @pl.when((n == 1) & first_core)
-        def _():
-            for pair, step in enumerate(send_order[:2]):
-                pl.semaphore_wait(gate.at[pair], 1)
-                for rank in range(CAP):
-                    a_copy(step, rank).start()
-
     def one_distance(n, carry):
         step = arrival(n)
-        if gated:
-            flow(n)
+        if paced:
+            @pl.when((n == 1) & first_core)
+            def _():
+                for rank in range(CAP):
+                    a_copy(send_order[0], rank).wait_send()
+                    a_copy(send_order[1], rank).start()
 
         slots = []
         lifts = [[] for _ in range(2 * coarse)]
@@ -297,7 +293,7 @@
             lift_cat.append(jnp.concatenate([high, low, high], axis=1))
         lift_cat = jnp.concatenate(lift_cat, axis=0)
 
-        def one_chunk(c, carry):
+        for c in range(chunks):
             halves = []
             for q in range(2):
                 w = 2 * c + q
@@ -306,6 +302,8 @@
                     total = None
                     for m in range(A_TILES * P_TILES):
                         k, p = m // P_TILES, m % P_TILES
+                        if not may_reach(k, p, w // coarse):
+                            continue
                         weight = jnp.where(slots[rank][m] == w, 1.0, 0.0)
                         term = weight * products[rank, k, :, pl.ds(p * tile, tile)]
                         total = term if total is None else total + term
@@ -326,9 +324,6 @@
             def _():
                 next_copy(c).start()
 
-            return carry
-
-        lax.fori_loop(0, chunks, one_chunk, 0)
         return carry
 
     lax.fori_loop(0, span, one_distance, 0)
@@ -337,8 +332,8 @@
         table_copy(step).wait_send()
     for step in send_order:
         for rank in range(CAP):
-            if gated and step is not send_order[2]:
-                @pl.when(first_core)
+            if paced and step is send_order[0]:
+                @pl.when(jnp.logical_not(first_core))
                 def _():
                     a_copy(step, rank).wait_send()
             else:
@@ -397,7 +392,6 @@
             dma((span, CAP)), dma((span, CAP)), dma((span,)), dma((span,)),
             dma((2,)), dma((2,)), dma((2,)), dma((2,)),
             dma((2 * coarse,)), dma((2 * coarse,)), dma((5,)),
-            pltpu.SemaphoreType.REGULAR((2,)),
         ],
         compiler_params=pltpu.CompilerParams(
             collective_id=0, has_side_effects=True, vmem_limit_bytes=48 * 1024 * 1024),

time: 61.9 us -> 60.3 us (0.974)
  the two profiles are of different devices: /device:TPU:12 before, /device:TPU:4 now
where the time goes in v6:
time: 60.3 us; the launch traced here: 60.2 us
  Pallas kernels  58.9 us (98%)
  other arithmetic  1.2 us (2%)
    pallas_call x1, Pallas kernels, shards(): pl.pallas_call(functools.partial(kernel, span, gx, gy), out_shape=[band_i...  58.9 us

profile of v6, /device:TPU:4, one launch (start us, length us, event | category | flops | bytes accessed | tf_op | source)
XLA Modules:
  0.0 60.2 jit_solution(4580386763687920360)
XLA Ops:
  0.0 58.9 %galerkin.1 = (f32[2,8,128,128]{3,2,1,0:T(8,128)S(1)}, f32[2,8,128,128]{3,2,1,0:T(8,128)S(1)}) custom-call(s32[8]{0:T(128)} %new_row_hbm.1, s32[4,8]{1,0:T(4,128)} %bitcast.2, s32[2,8]{1,0:T(2,128)} %bitcast.3, f32[8,4,128,128]{3,2,1,0:T(8,128)} %a_hbm.1, f32[8,2,128,128]{3,2,1,0:T(8,128)} %p_hbm.1), custom_call_target="tpu_custom_call" | custom-call | tf_op jit(solution)/shard_map/galerkin/pallas_call | solution.py:369
  59.0 1.2 %pad_add_fusion = f32[2,10,128,128]{3,2,1,0:T(8,128)} fusion(f32[2,8,128,128]{3,2,1,0:T(8,128)S(1)} %get-tuple-element.8, f32[2,8,128,128]{3,2,1,0:T(8,128)S(1)} %get-tuple-element.7), kind=kLoop, calls=%fused_computation | loop fusion | flops 327680 | bytes 3407872 | tf_op jit(solution)/shard_map/add | solution.py:402

commit v7 on v2

--- a/solution.py
+++ b/solution.py
@@ -32,14 +32,21 @@
     return found, seen > rank
 
 
+def may_reach(k, p, place):
+    columns = (1,) if k == 0 else (0, 1, 2)
+    if p == 0:
+        return place in columns
+    return place - 1 in columns or place == 1
+
+
 def kernel(
     span, gx, gy,
     new_row_hbm, a_cols_hbm, p_cols_hbm, a_hbm, p_hbm,
-    own_out, arrived_ref,
-    own_ref, new_row_ref, a_cols_ref, p_cols_ref, a_ref, p_ref,
+    own_ref, arrived_ref,
+    new_row_ref, a_cols_ref, p_cols_ref, a_ref, p_ref,
     stage, recv, ext, ext_cat, flipped, products, following,
     table, table_from, table_ext, from_s, ext_s,
-    a_send, a_recv, t_send, t_recv, h_send, h_recv, ht_send, ht_recv, n_send, n_recv, local_sem, gate, o_sem,
+    a_send, a_recv, t_send, t_recv, h_send, h_recv, ht_send, ht_recv, n_send, n_recv, local_sem, gate,
 ):
     rows, tile = p_ref.shape[0], p_ref.shape[2]
     coarse = rows // 4
@@ -231,10 +238,6 @@
         return pltpu.make_async_remote_copy(
             following.at[:, piece], arrived_ref.at[:, piece], n_send.at[n], n_recv.at[n],
             device_id={"gy": y + 1}, device_id_type=pl.DeviceIdType.MESH)
-
-    def own_copy(n):
-        piece = pl.ds(2 * n, 2)
-        return pltpu.make_async_copy(own_ref.at[:, piece], own_out.at[:, piece], o_sem.at[n])
 
     def one_distance(n, carry):
         step = arrival(n)
@@ -285,7 +288,7 @@
             lift_cat.append(jnp.concatenate([high, low, high], axis=1))
         lift_cat = jnp.concatenate(lift_cat, axis=0)
 
-        def one_chunk(c, carry):
+        for c in range(chunks):
             halves = []
             for q in range(2):
                 w = 2 * c + q
@@ -294,6 +297,8 @@
                     total = None
                     for m in range(A_TILES * P_TILES):
                         k, p = m // P_TILES, m % P_TILES
+                        if not may_reach(k, p, w // coarse):
+                            continue
                         weight = jnp.where(slots[rank][m] == w, 1.0, 0.0)
                         term = weight * products[rank, k, :, pl.ds(p * tile, tile)]
                         total = term if total is None else total + term
@@ -314,13 +319,6 @@
             def _():
                 next_copy(c).start()
 
-            @pl.when(n == span - 1)
-            def _():
-                own_copy(c).start()
-
-            return carry
-
-        lax.fori_loop(0, chunks, one_chunk, 0)
         return carry
 
     lax.fori_loop(0, span, one_distance, 0)
@@ -338,9 +336,6 @@
         for step in send_order:
             a_copy(step).wait_send()
 
-    for c in range(chunks):
-        own_copy(c).wait()
-
     @pl.when(has_right)
     def _():
         for copy in halo_copies(0):
@@ -362,15 +357,18 @@
     span = min(SPAN, gx)
     coarse = rows // 4
     band = jax.ShapeDtypeStruct((coarse, 4 * coarse, tile, tile), jnp.float32)
+    band_in = pltpu.VMEM(band.shape, jnp.float32)
     dma = pltpu.SemaphoreType.DMA
     row_block = (span, CAP, A_TILES, tile, tile)
+    operands = [
+        pltpu.with_memory_space_constraint(value, pltpu.HBM)
+        for value in (new_row, a_cols.T, p_cols.T, a_tiles, p_tiles)]
     own, arrived = pl.pallas_call(
         functools.partial(kernel, span, gx, gy),
-        out_shape=[band, band],
+        out_shape=[band_in, band_in],
         in_specs=[pl.BlockSpec(memory_space=pl.ANY)] * 5,
-        out_specs=[pl.BlockSpec(memory_space=pl.ANY)] * 2,
+        out_specs=[pl.BlockSpec(memory_space=pltpu.VMEM)] * 2,
         scratch_shapes=[
-            pltpu.VMEM(band.shape, jnp.float32),
             pltpu.SMEM((rows,), jnp.int32),
             pltpu.SMEM((A_TILES, rows), jnp.int32),
             pltpu.SMEM((P_TILES, rows), jnp.int32),
@@ -391,12 +389,12 @@
             dma((span,)), dma((span,)), dma((span,)), dma((span,)),
             dma((2,)), dma((2,)), dma((2,)), dma((2,)),
             dma((2 * coarse,)), dma((2 * coarse,)), dma((5,)),
-            pltpu.SemaphoreType.REGULAR, dma((2 * coarse,)),
+            pltpu.SemaphoreType.REGULAR,
         ],
         compiler_params=pltpu.CompilerParams(
-            collective_id=0, has_side_effects=True, vmem_limit_bytes=64 * 1024 * 1024),
+            collective_id=0, has_side_effects=True, vmem_limit_bytes=48 * 1024 * 1024),
         name="galerkin",
-    )(new_row, a_cols.T, p_cols.T, a_tiles, p_tiles)
+    )(*operands)
     pad = ((0, 0), (coarse, 0), (0, 0), (0, 0))
     behind = ((0, 0), (0, coarse), (0, 0), (0, 0))
     return jnp.pad(own, pad) + jnp.pad(arrived, behind)

time: 60.1 us -> 59.4 us (0.988)
  other arithmetic: 2.74 us -> 1.2 us
    add x1, other arithmetic: 2.74 us -> 1.2 us  [shards(): return jnp.pad(own, pad) + jnp.pad(arrived, behind)]
where the time goes in v7:
time: 59.4 us; the launch traced here: 58.7 us
  Pallas kernels  57.5 us (97%)
  other arithmetic  1.2 us (2%)
    pallas_call x1, Pallas kernels, shards(): pl.pallas_call(functools.partial(kernel, span, gx, gy), out_shape=[band_i...  57.5 us
    add x1, other arithmetic, shards(): return jnp.pad(own, pad) + jnp.pad(arrived, behind)  1.2 us

profile of v7, /device:TPU:12, one launch (start us, length us, event | category | flops | bytes accessed | tf_op | source)
XLA Modules:
  0.0 58.7 jit_solution(11535261125793171620)
XLA Ops:
  0.0 57.5 %galerkin.1 = (f32[2,8,128,128]{3,2,1,0:T(8,128)S(1)}, f32[2,8,128,128]{3,2,1,0:T(8,128)S(1)}) custom-call(s32[8]{0:T(128)} %new_row_hbm.1, s32[4,8]{1,0:T(4,128)} %bitcast.2, s32[2,8]{1,0:T(2,128)} %bitcast.3, f32[8,4,128,128]{3,2,1,0:T(8,128)} %a_hbm.1, f32[8,2,128,128]{3,2,1,0:T(8,128)} %p_hbm.1), custom_call_target="tpu_custom_call" | custom-call | tf_op jit(solution)/shard_map/galerkin/pallas_call | solution.py:366
  57.5 1.2 %pad_add_fusion = f32[2,10,128,128]{3,2,1,0:T(8,128)} fusion(f32[2,8,128,128]{3,2,1,0:T(8,128)S(1)} %get-tuple-element.8, f32[2,8,128,128]{3,2,1,0:T(8,128)S(1)} %get-tuple-element.7), kind=kLoop, calls=%fused_computation | loop fusion | flops 327680 | bytes 3407872 | tf_op jit(solution)/shard_map/add | solution.py:400

commit v8 on v7

--- a/solution.py
+++ b/solution.py
@@ -61,8 +61,8 @@
     inputs = [
         pltpu.make_async_copy(source, target, local_sem.at[n])
         for n, (source, target) in enumerate((
-            (new_row_hbm, new_row_ref), (a_cols_hbm, a_cols_ref), (p_cols_hbm, p_cols_ref),
-            (a_hbm, a_ref), (p_hbm, p_ref)))]
+            (a_hbm, a_ref), (new_row_hbm, new_row_ref), (a_cols_hbm, a_cols_ref),
+            (p_cols_hbm, p_cols_ref), (p_hbm, p_ref)))]
     for copy in inputs:
         copy.start()
 
@@ -82,7 +82,7 @@
         pl.semaphore_signal(
             barrier, inc=1, device_id={"gy": y + 1}, device_id_type=pl.DeviceIdType.MESH)
 
-    for copy in inputs[:3]:
+    for copy in inputs[1:4]:
         copy.wait()
     row_id = lax.broadcasted_iota(jnp.int32, (rows, LANES), 0)
     lane_id = lax.broadcasted_iota(jnp.int32, (rows, LANES), 1)
@@ -127,20 +127,23 @@
 
     if gx == 4 and span == 4:
         odd = lax.rem(x, 2)
-        send_order = [2, 3 - 2 * odd, 1 + 2 * odd]
+        core = lax.rem(y, 2)
+        beside = 1 + 2 * odd
+        send_order = [2 * (1 - core) + beside * core, beside * (1 - core) + 2 * core, 4 - beside]
+        came = 3 - 2 * odd
+        came_order = [2 * (1 - core) + came * core, came * (1 - core) + 2 * core, 4 - came]
 
         def arrival(n):
-            later = n // 2
-            return 2 * n * (1 - later) + later * (
-                (1 - odd) * (3 - 2 * (n - 2)) + odd * (1 + 2 * (n - 2)))
+            low, high = lax.rem(n, 2), n // 2
+            return (came_order[0] * low * (1 - high) + came_order[1] * (1 - low) * high
+                    + came_order[2] * low * high)
     else:
         send_order = list(range(1, span))
 
         def arrival(n):
             return n
 
-    for copy in inputs[3:]:
-        copy.wait()
+    inputs[0].wait()
     put_rows(send_order[0], stage, send_order[0])
     greeted = span - 1 + jnp.where(has_left, 1, 0) + jnp.where(has_right, 1, 0)
     pl.semaphore_wait(barrier, greeted)
@@ -158,9 +161,9 @@
         for copy in halo_copies(1):
             copy.start()
 
-    for n, step in enumerate(send_order[1:]):
+    for step in send_order[1:]:
         put_rows(step, stage, step)
-        if gated and n == 0:
+        if gated and step is send_order[2]:
             @pl.when(jnp.logical_not(first_core))
             def _():
                 a_copy(step).start()
@@ -184,6 +187,7 @@
             flipped[row, q] = p_ref[row, q].T
         return carry
 
+    inputs[4].wait()
     lax.fori_loop(0, rows, flip, 0)
     split_p(p_ref, rows)
 
@@ -242,14 +246,14 @@
     def one_distance(n, carry):
         step = arrival(n)
         if gated:
-            @pl.when((n == 1) & first_core)
+            @pl.when((n == span - 1) & first_core)
             def _():
                 pl.semaphore_wait(gate, 1)
-                a_copy(send_order[1]).start()
-
-            @pl.when((n == 1) & jnp.logical_not(first_core))
+                a_copy(send_order[2]).start()
+
+            @pl.when((n == span - 1) & jnp.logical_not(first_core))
             def _():
-                for sent in send_order[:2]:
+                for sent in send_order[1:]:
                     a_copy(sent).wait_send()
                 pl.semaphore_signal(
                     gate, inc=1, device_id={"gy": y - 1}, device_id_type=pl.DeviceIdType.MESH)
@@ -325,15 +329,14 @@
 
     for step in range(1, span):
         table_copy(step).wait_send()
+    a_copy(send_order[0]).wait_send()
     if gated:
         @pl.when(first_core)
         def _():
-            for step in send_order[:2]:
+            for step in send_order[1:]:
                 a_copy(step).wait_send()
-
-        a_copy(send_order[2]).wait_send()
     else:
-        for step in send_order:
+        for step in send_order[1:]:
             a_copy(step).wait_send()
 
     @pl.when(has_right)

time: 59.4 us -> 63.9 us (1.076)
  Pallas kernels: 57.5 us -> 62 us
    pallas_call x1, Pallas kernels: 57.5 us -> 62 us  [shards(): pl.pallas_call(functools.partial(kernel, span, gx, gy), out_shape=[band_i...]
where the time goes in v8:
time: 63.9 us; the launch traced here: 63.2 us
  Pallas kernels  62 us (97%)
  other arithmetic  1.2 us (2%)
    pallas_call x1, Pallas kernels, shards(): pl.pallas_call(functools.partial(kernel, span, gx, gy), out_shape=[band_i...  62 us

profile of v8, /device:TPU:12, one launch (start us, length us, event | category | flops | bytes accessed | tf_op | source)
XLA Modules:
  0.0 63.2 jit_solution(14775250915567344259)
XLA Ops:
  0.0 62.0 %galerkin.1 = (f32[2,8,128,128]{3,2,1,0:T(8,128)S(1)}, f32[2,8,128,128]{3,2,1,0:T(8,128)S(1)}) custom-call(s32[8]{0:T(128)} %new_row_hbm.1, s32[4,8]{1,0:T(4,128)} %bitcast.2, s32[2,8]{1,0:T(2,128)} %bitcast.3, f32[8,4,128,128]{3,2,1,0:T(8,128)} %a_hbm.1, f32[8,2,128,128]{3,2,1,0:T(8,128)} %p_hbm.1), custom_call_target="tpu_custom_call" | custom-call | tf_op jit(solution)/shard_map/galerkin/pallas_call | solution.py:369
  62.0 1.2 %pad_add_fusion = f32[2,10,128,128]{3,2,1,0:T(8,128)} fusion(f32[2,8,128,128]{3,2,1,0:T(8,128)S(1)} %get-tuple-element.8, f32[2,8,128,128]{3,2,1,0:T(8,128)S(1)} %get-tuple-element.7), kind=kLoop, calls=%fused_computation | loop fusion | flops 327680 | bytes 3407872 | tf_op jit(solution)/shard_map/add | solution.py:403

commit v9 on v8

--- a/solution.py
+++ b/solution.py
@@ -246,12 +246,12 @@
     def one_distance(n, carry):
         step = arrival(n)
         if gated:
-            @pl.when((n == span - 1) & first_core)
+            @pl.when((n == 2) & first_core)
             def _():
                 pl.semaphore_wait(gate, 1)
                 a_copy(send_order[2]).start()
 
-            @pl.when((n == span - 1) & jnp.logical_not(first_core))
+            @pl.when((n == 2) & jnp.logical_not(first_core))
             def _():
                 for sent in send_order[1:]:
                     a_copy(sent).wait_send()

time: 63.9 us -> 61 us (0.955)
  Pallas kernels: 62 us -> 59.1 us
    pallas_call x1, Pallas kernels: 62 us -> 59.1 us  [shards(): pl.pallas_call(functools.partial(kernel, span, gx, gy), out_shape=[band_i...]
where the time goes in v9:
time: 61 us; the launch traced here: 60.3 us
  Pallas kernels  59.1 us (97%)
  other arithmetic  1.2 us (2%)
    pallas_call x1, Pallas kernels, shards(): pl.pallas_call(functools.partial(kernel, span, gx, gy), out_shape=[band_i...  59.1 us

profile of v9, /device:TPU:12, one launch (start us, length us, event | category | flops | bytes accessed | tf_op | source)
XLA Modules:
  0.0 60.3 jit_solution(5072273748230196042)
XLA Ops:
  0.0 59.1 %galerkin.1 = (f32[2,8,128,128]{3,2,1,0:T(8,128)S(1)}, f32[2,8,128,128]{3,2,1,0:T(8,128)S(1)}) custom-call(s32[8]{0:T(128)} %new_row_hbm.1, s32[4,8]{1,0:T(4,128)} %bitcast.2, s32[2,8]{1,0:T(2,128)} %bitcast.3, f32[8,4,128,128]{3,2,1,0:T(8,128)} %a_hbm.1, f32[8,2,128,128]{3,2,1,0:T(8,128)} %p_hbm.1), custom_call_target="tpu_custom_call" | custom-call | tf_op jit(solution)/shard_map/galerkin/pallas_call | solution.py:369
  59.1 1.2 %pad_add_fusion = f32[2,10,128,128]{3,2,1,0:T(8,128)} fusion(f32[2,8,128,128]{3,2,1,0:T(8,128)S(1)} %get-tuple-element.8, f32[2,8,128,128]{3,2,1,0:T(8,128)S(1)} %get-tuple-element.7), kind=kLoop, calls=%fused_computation | loop fusion | flops 327680 | bytes 3407872 | tf_op jit(solution)/shard_map/add | solution.py:403

commit v10 on v7

--- a/solution.py
+++ b/solution.py
@@ -61,8 +61,8 @@
     inputs = [
         pltpu.make_async_copy(source, target, local_sem.at[n])
         for n, (source, target) in enumerate((
-            (new_row_hbm, new_row_ref), (a_cols_hbm, a_cols_ref), (p_cols_hbm, p_cols_ref),
-            (a_hbm, a_ref), (p_hbm, p_ref)))]
+            (a_hbm, a_ref), (new_row_hbm, new_row_ref), (a_cols_hbm, a_cols_ref),
+            (p_cols_hbm, p_cols_ref), (p_hbm, p_ref)))]
     for copy in inputs:
         copy.start()
 
@@ -82,7 +82,7 @@
         pl.semaphore_signal(
             barrier, inc=1, device_id={"gy": y + 1}, device_id_type=pl.DeviceIdType.MESH)
 
-    for copy in inputs[:3]:
+    for copy in inputs[1:4]:
         copy.wait()
     row_id = lax.broadcasted_iota(jnp.int32, (rows, LANES), 0)
     lane_id = lax.broadcasted_iota(jnp.int32, (rows, LANES), 1)
@@ -139,8 +139,7 @@
         def arrival(n):
             return n
 
-    for copy in inputs[3:]:
-        copy.wait()
+    inputs[0].wait()
     put_rows(send_order[0], stage, send_order[0])
     greeted = span - 1 + jnp.where(has_left, 1, 0) + jnp.where(has_right, 1, 0)
     pl.semaphore_wait(barrier, greeted)
@@ -184,6 +183,7 @@
             flipped[row, q] = p_ref[row, q].T
         return carry
 
+    inputs[4].wait()
     lax.fori_loop(0, rows, flip, 0)
     split_p(p_ref, rows)
 
@@ -247,7 +247,7 @@
                 pl.semaphore_wait(gate, 1)
                 a_copy(send_order[1]).start()
 
-            @pl.when((n == 1) & jnp.logical_not(first_core))
+            @pl.when((n == 2) & jnp.logical_not(first_core))
             def _():
                 for sent in send_order[:2]:
                     a_copy(sent).wait_send()

time: 59.4 us -> 59.5 us (level)
  the two profiles are of different devices: /device:TPU:12 before, /device:TPU:4 now
where the time goes in v10:
time: 59.5 us; the launch traced here: 59.3 us
  Pallas kernels  58.1 us (98%)
  other arithmetic  1.2 us (2%)
    pallas_call x1, Pallas kernels, shards(): pl.pallas_call(functools.partial(kernel, span, gx, gy), out_shape=[band_i...  58.1 us
    add x1, other arithmetic, shards(): return jnp.pad(own, pad) + jnp.pad(arrived, behind)  1.2 us

profile of v10, /device:TPU:4, one launch (start us, length us, event | category | flops | bytes accessed | tf_op | source)
XLA Modules:
  0.0 59.3 jit_solution(8521065693508236755)
XLA Ops:
  0.0 58.1 %galerkin.1 = (f32[2,8,128,128]{3,2,1,0:T(8,128)S(1)}, f32[2,8,128,128]{3,2,1,0:T(8,128)S(1)}) custom-call(s32[8]{0:T(128)} %new_row_hbm.1, s32[4,8]{1,0:T(4,128)} %bitcast.2, s32[2,8]{1,0:T(2,128)} %bitcast.3, f32[8,4,128,128]{3,2,1,0:T(8,128)} %a_hbm.1, f32[8,2,128,128]{3,2,1,0:T(8,128)} %p_hbm.1), custom_call_target="tpu_custom_call" | custom-call | tf_op jit(solution)/shard_map/galerkin/pallas_call | solution.py:366
  58.1 1.2 %pad_add_fusion = f32[2,10,128,128]{3,2,1,0:T(8,128)} fusion(f32[2,8,128,128]{3,2,1,0:T(8,128)S(1)} %get-tuple-element.8, f32[2,8,128,128]{3,2,1,0:T(8,128)S(1)} %get-tuple-element.7), kind=kLoop, calls=%fused_computation | loop fusion | flops 327680 | bytes 3407872 | tf_op jit(solution)/shard_map/add | solution.py:400
